TPU v7x, 32 devices: a whole 2x2x4 slice. The times are simulated.
32 devices in a mesh: obj: 4 (over y, core), scan: 8 (over z, x).
Axes of the slice: x: 2, y: 2, z: 4, core: 2. Of those that a mesh axis runs over, the one named last changes fastest.
Arguments:
- object_slab: float32 [2, 2, 1536, 4096], P(None, None, 'obj', 'scan'), may hold values from -4 to 4
- probe_mode_stack: float32 [6, 2, 256, 256], replicated, may hold values from -2 to 2
- offsets: int32 [96, 2], P(('obj', 'scan')), may hold values from 0 to 3840, as said below
- measured: float32 [96, 256, 256], P(('obj', 'scan')), may hold values from 0.05 to 3
- counts: int32 [32], P(('obj', 'scan')), may hold values from 1 to 3, as said below
Outputs:
- new_object: float32 [2, 2, 1536, 4096], P(None, None, 'obj', 'scan')
- new_probe: float32 [6, 2, 256, 256], replicated
Inputs may be any that keep to these rules, and one draw needn't show every extreme that they name: `offsets`: rows 3 d to 3 d + 2 belong to device d (devices in the order obj, then scan). Each row gives the object row and column of a patch's top-left pixel; that pixel lies in the device's own tile of 384 x 512 pixels, and the whole 256 x 256 patch lies inside the object. Device d uses its first counts[d] position slots; the others are ignored.
All inputs are finite; a program needn't handle non-finite values.
Results may differ from a plain program's by a relative error of at most 0.008.
The roundings to bfloat16 on the way count: a program that leaves them out, or rounds other values in their place, can miss the bound.
Values sent between devices are 32-bit elements; how exact they have to be, the bound alone decides.
A program may use at most 128 MiB of HBM per device.

v0:
```python
import functools
import math

import jax
import jax.numpy as jnp
import numpy as np
from jax import lax
from jax.experimental import pallas as pl
from jax.experimental.pallas import tpu as pltpu
from jax.sharding import PartitionSpec as P

chirp_scale = 24.0
probe_step = 0.15
lanes = 128
sublanes = 8
vmem_bytes = 56 * 1024 * 1024


def from_behind(array, axis, by):
    count = lax.axis_size(axis)
    pairs = [(i, i + by) for i in range(count) if 0 <= i + by < count]
    return lax.ppermute(array, axis, pairs)


def dft_matrix(pattern, sign_factor):
    indices = np.arange(pattern)
    angles = (indices[:, None] * indices[None, :] % pattern) * (2.0 * math.pi / pattern)
    real_part = np.cos(angles) / math.sqrt(pattern)
    imag_part = sign_factor * np.sin(angles) / math.sqrt(pattern)
    upper = np.concatenate([real_part, -imag_part], axis=1)
    lower = np.concatenate([imag_part, real_part], axis=1)
    return jnp.asarray(np.concatenate([upper, lower], axis=0).astype(np.float32), jnp.bfloat16)


def propagator(pattern):
    indices = np.arange(pattern)
    freqs = ((indices + pattern // 2) % pattern - pattern // 2) / pattern
    phases = -math.pi * chirp_scale * (freqs[:, None] ** 2 + freqs[None, :] ** 2)
    return jnp.asarray(np.stack([np.cos(phases), np.sin(phases)], axis=0).astype(np.float32))


def aligned(row, col):
    row_base = pl.multiple_of(row // sublanes * sublanes, sublanes)
    col_base = pl.multiple_of(col // lanes * lanes, lanes)
    return row_base, col_base, row - row_base, col - col_base


def pad(array):
    array = jnp.concatenate([array, jnp.zeros((array.shape[0], lanes), jnp.float32)], axis=1)
    return jnp.concatenate([array, jnp.zeros((sublanes, array.shape[1]), jnp.float32)], axis=0)


def roll_down(array, rows, cols):
    return pltpu.roll(pltpu.roll(array, cols, 1), rows, 0)


def transform(real_part, imag_part, left, right):
    pattern = real_part.shape[0]
    stacked = jnp.concatenate([real_part.astype(jnp.bfloat16), imag_part.astype(jnp.bfloat16)], axis=0)
    half = jnp.dot(left, stacked, preferred_element_type=jnp.float32).astype(jnp.bfloat16)
    half = jnp.concatenate([half[:pattern], half[pattern:]], axis=1)
    full = jnp.dot(half, right, preferred_element_type=jnp.float32)
    return full[:, :pattern], full[:, pattern:]


def slots_kernel(
    corners, used, tile, right, lower, corner, probe, measured, table_f, table_b, fresnel,
    grad_tile, grad_right, grad_lower, grad_corner, grad_probe,
    ext, grad, window, waves, far, intensity, term, sems_in, sems_out,
):
    modes, _, pattern, _ = probe.shape
    layers = tile.shape[0]
    height, width = tile.shape[2], tile.shape[3]
    wide = pattern + lanes
    tall = pattern + sublanes

    def spots(buffer):
        return (
            buffer.at[:, :, pl.ds(0, height), pl.ds(0, width)],
            buffer.at[:, :, pl.ds(0, height), pl.ds(width, pattern)],
            buffer.at[:, :, pl.ds(height, pattern), pl.ds(0, width)],
            buffer.at[:, :, pl.ds(height, pattern), pl.ds(width, pattern)],
        )

    loads = [
        pltpu.make_async_copy(source, spot, sems_in.at[k])
        for k, (source, spot) in enumerate(zip((tile, right, lower, corner), spots(ext)))
    ]
    for load in loads:
        load.start()
    grad[...] = jnp.zeros_like(grad)
    grad_probe[...] = jnp.zeros_like(grad_probe)
    for load in loads:
        load.wait()

    @pl.loop(0, used[0])
    def _(slot):
        row = corners[slot, 0]
        col = corners[slot, 1]
        row_base, col_base, row_shift, col_shift = aligned(row, col)
        row_back = jnp.where(row_shift == 0, 0, tall - row_shift)
        col_back = jnp.where(col_shift == 0, 0, wide - col_shift)
        for layer in range(layers):
            for part in range(2):
                block = ext[layer, part, pl.ds(row_base, tall), pl.ds(col_base, wide)]
                window[layer, part] = roll_down(block, row_back, col_back)[:pattern, :pattern]
        intensity[...] = jnp.zeros_like(intensity)
        term[...] = jnp.zeros_like(term)

        @pl.loop(0, modes, unroll=2)
        def _(mode):
            wr, wi = probe[mode, 0], probe[mode, 1]
            for layer in range(layers):
                o_r, o_i = window[layer, 0], window[layer, 1]
                fr, fi = transform(o_r * wr - o_i * wi, o_r * wi + o_i * wr, table_f[...], table_b[...])
                if layer < layers - 1:
                    hr, hi = fresnel[0], fresnel[1]
                    wr, wi = transform(hr * fr - hi * fi, hr * fi + hi * fr, table_b[...], table_f[...])
                    waves[layer, mode, 0] = wr
                    waves[layer, mode, 1] = wi
            far[mode, 0] = fr
            far[mode, 1] = fi
            intensity[...] += fr * fr + fi * fi

        intensity[...] = intensity[...] - measured[slot]

        @pl.loop(0, modes, unroll=2)
        def _(mode):
            gain = intensity[...]
            gr, gi = transform(gain * far[mode, 0], gain * far[mode, 1], table_b[...], table_f[...])
            for layer in reversed(range(layers)):
                if layer < layers - 1:
                    sr, si = transform(gr, gi, table_f[...], table_b[...])
                    hr, hi = fresnel[0], fresnel[1]
                    gr, gi = transform(hr * sr + hi * si, hr * si - hi * sr, table_b[...], table_f[...])
                if layer == 0:
                    wr, wi = probe[mode, 0], probe[mode, 1]
                else:
                    wr, wi = waves[layer - 1, mode, 0], waves[layer - 1, mode, 1]
                term[layer, 0] += wr * gr + wi * gi
                term[layer, 1] += wr * gi - wi * gr
                o_r, o_i = window[layer, 0], window[layer, 1]
                gr, gi = o_r * gr + o_i * gi, o_r * gi - o_i * gr
            grad_probe[mode, 0] += gr
            grad_probe[mode, 1] += gi

        for layer in range(layers):
            for part in range(2):
                at = (layer, part, pl.ds(row_base, tall), pl.ds(col_base, wide))
                grad[at] = grad[at] + roll_down(pad(term[layer, part]), row_shift, col_shift)

    saves = [
        pltpu.make_async_copy(spot, target, sems_out.at[k])
        for k, (spot, target) in enumerate(
            zip(spots(grad), (grad_tile, grad_right, grad_lower, grad_corner))
        )
    ]
    for save in saves:
        save.start()
    for save in saves:
        save.wait()


def run_slots(corners, used, tile, right, lower, corner, probe, measured, table_f, table_b, fresnel):
    layers, _, height, width = tile.shape
    modes, _, pattern, _ = probe.shape
    smem = pl.BlockSpec(memory_space=pltpu.SMEM)
    vmem = pl.BlockSpec(memory_space=pltpu.VMEM)
    anyw = pl.BlockSpec(memory_space=pl.ANY)
    f32 = jnp.float32
    ext_shape = (layers, 2, height + pattern, width + pattern)
    return pl.pallas_call(
        slots_kernel,
        out_shape=(
            jax.ShapeDtypeStruct(tile.shape, f32),
            jax.ShapeDtypeStruct(right.shape, f32),
            jax.ShapeDtypeStruct(lower.shape, f32),
            jax.ShapeDtypeStruct(corner.shape, f32),
            jax.ShapeDtypeStruct(probe.shape, f32),
        ),
        in_specs=[smem, smem, anyw, anyw, anyw, anyw, vmem, vmem, vmem, vmem, vmem],
        out_specs=(anyw, anyw, anyw, anyw, vmem),
        scratch_shapes=[
            pltpu.VMEM(ext_shape, f32),
            pltpu.VMEM(ext_shape, f32),
            pltpu.VMEM((layers, 2, pattern, pattern), f32),
            pltpu.VMEM((layers - 1, modes, 2, pattern, pattern), f32),
            pltpu.VMEM((modes, 2, pattern, pattern), f32),
            pltpu.VMEM((pattern, pattern), f32),
            pltpu.VMEM((layers, 2, pattern, pattern), f32),
            pltpu.SemaphoreType.DMA((4,)),
            pltpu.SemaphoreType.DMA((4,)),
        ],
        compiler_params=pltpu.CompilerParams(vmem_limit_bytes=vmem_bytes),
        cost_estimate=pl.CostEstimate(flops=29_000_000_000, bytes_accessed=30_000_000, transcendentals=0),
    )(corners, used, tile, right, lower, corner, probe, measured, table_f, table_b, fresnel)


def light_kernel(height, width, slots, info, probe, light, canvas, power):
    modes, _, pattern, _ = probe.shape
    total = jnp.zeros((pattern, pattern), jnp.float32)
    for mode in range(modes):
        total = total + (probe[mode, 0] * probe[mode, 0] + probe[mode, 1] * probe[mode, 1])
    power[...] = pad(total)
    canvas[...] = jnp.zeros_like(canvas)
    for block in range(4):
        base = block * (2 * slots + 1)

        @pl.loop(0, info[base + 2 * slots])
        def _(slot):
            row = info[base + 2 * slot] + height
            col = info[base + 2 * slot + 1] + width
            row_base, col_base, row_shift, col_shift = aligned(row, col)
            at = (pl.ds(row_base, pattern + sublanes), pl.ds(col_base, pattern + lanes))
            canvas[at] = canvas[at] + roll_down(power[...], row_shift, col_shift)

    light[...] = canvas[height : 2 * height, width : 2 * width] + 1.0


def run_light(height, width, slots, info, probe):
    pattern = probe.shape[-1]
    return pl.pallas_call(
        functools.partial(light_kernel, height, width, slots),
        out_shape=jax.ShapeDtypeStruct((height, width), jnp.float32),
        in_specs=[pl.BlockSpec(memory_space=pltpu.SMEM), pl.BlockSpec(memory_space=pltpu.VMEM)],
        out_specs=pl.BlockSpec(memory_space=pltpu.VMEM),
        scratch_shapes=[
            pltpu.VMEM((2 * height + pattern, 2 * width + pattern), jnp.float32),
            pltpu.VMEM((pattern + sublanes, pattern + lanes), jnp.float32),
        ],
        compiler_params=pltpu.CompilerParams(vmem_limit_bytes=24 * 1024 * 1024),
        cost_estimate=pl.CostEstimate(flops=10_000_000, bytes_accessed=12_000_000, transcendentals=0),
    )(info, probe)


def final_kernel(tile, grad, left, above, corner, light, out):
    pattern = left.shape[-1]
    grad[0, 0, :, :pattern] = grad[0, 0, :, :pattern] + left[0, 0]
    grad[0, 0, :pattern, :] = grad[0, 0, :pattern, :] + above[0, 0]
    grad[0, 0, :pattern, :pattern] = grad[0, 0, :pattern, :pattern] + corner[0, 0]
    out[0, 0] = tile[0, 0] - grad[0, 0] / light[...]


def run_final(tile, grad, left, above, corner, light):
    layers, parts, height, width = tile.shape
    spec = lambda array: pl.BlockSpec((1, 1) + array.shape[2:], lambda i, j: (i, j, 0, 0))
    return pl.pallas_call(
        final_kernel,
        grid=(layers, parts),
        out_shape=jax.ShapeDtypeStruct(tile.shape, jnp.float32),
        in_specs=[
            spec(tile), spec(grad), spec(left), spec(above), spec(corner),
            pl.BlockSpec(light.shape, lambda i, j: (0, 0)),
        ],
        out_specs=spec(tile),
        compiler_params=pltpu.CompilerParams(vmem_limit_bytes=24 * 1024 * 1024),
        cost_estimate=pl.CostEstimate(flops=4_000_000, bytes_accessed=14_000_000, transcendentals=0),
    )(tile, grad, left, above, corner, light)


def on_device(object_slab, probe_mode_stack, offsets, measured, counts):
    tile_height = object_slab.shape[2]
    tile_width = object_slab.shape[3]
    pattern = probe_mode_stack.shape[-1]
    slots = offsets.shape[0]
    table_f = dft_matrix(pattern, -1.0)
    table_b = dft_matrix(pattern, 1.0)
    fresnel = propagator(pattern)
    right_rim = from_behind(object_slab[:, :, :, :pattern], "scan", -1)
    lower_rim = from_behind(object_slab[:, :, :pattern, :], "obj", -1)
    corner_rim = from_behind(right_rim[:, :, :pattern, :], "obj", -1)
    base = jnp.stack([lax.axis_index("obj") * tile_height, lax.axis_index("scan") * tile_width])
    base = base.astype(jnp.int32)
    corners = offsets - base
    own_info = jnp.concatenate([offsets.reshape(-1), counts])
    left_info = from_behind(own_info, "scan", 1)
    row_info = jnp.concatenate([own_info, left_info])
    info = jnp.concatenate([row_info, from_behind(row_info, "obj", 1)])
    right_rim, lower_rim, corner_rim, corners, info = lax.optimization_barrier(
        (right_rim, lower_rim, corner_rim, corners, info)
    )
    shifts = jnp.tile(jnp.concatenate([jnp.tile(base, slots), jnp.zeros((1,), jnp.int32)]), 4)
    light = run_light(tile_height, tile_width, slots, info - shifts, probe_mode_stack)
    grad_tile, grad_right, grad_lower, grad_corner, grad_probe = run_slots(
        corners, counts, object_slab, right_rim, lower_rim, corner_rim, probe_mode_stack,
        measured, table_f, table_b, fresnel,
    )
    summed = lax.psum(grad_probe, ("obj", "scan"))
    corner_half = from_behind(grad_corner, "obj", 1)
    from_above = from_behind(grad_lower, "obj", 1)
    from_left = from_behind(grad_right, "scan", 1)
    from_corner = from_behind(corner_half, "scan", 1)
    new_object = run_final(object_slab, grad_tile, from_left, from_above, from_corner, light)
    summed, new_object = lax.optimization_barrier((summed, new_object))
    grad_scale = jnp.sqrt(jnp.mean(summed * summed) + 1e-06)
    new_probe = probe_mode_stack - probe_step * summed / grad_scale
    return (new_object, new_probe)


def solution(mesh):
    in_specs = (
        P(None, None, "obj", "scan"),
        P(),
        P(("obj", "scan"), None),
        P(("obj", "scan"), None, None),
        P(("obj", "scan")),
    )
    out_specs = (P(None, None, "obj", "scan"), P())
    return jax.shard_map(
        on_device, mesh=mesh, in_specs=in_specs, out_specs=out_specs, check_vma=False
    )
```

profile of v0, /device:TPU:17, one launch (start us, length us, event | category | flops | bytes accessed | tf_op | source)
XLA Modules:
  0.0 314.6 jit_solution(4756519436662767817)
XLA Ops:
  7.2 0.0 copy-start
  7.2 0.0 all-reduce.2.cloned.1.call-start
  7.2 1.7 slice.9
  8.9 0.0 copy-start.6
  8.9 3.0 collective-permute-start
  11.9 0.0 copy-done
  11.9 1.5 slice.10
  13.4 2.9 collective-permute-start.1
  16.3 29.8 %collective-permute-done.right = f32[2,2,384,256]{3,2,1,0:T(8,128)S(1)} collective-permute-done((f32[2,2,384,256]{3,2,1,0:T(8,128)S(1)}, f32[2,2,384,256]{3,2,1,0:T(8,128)S(1)}, u32[]{:S(2)}, u32[]{:S(2)}) %collective-permute-start) | collective-permute-done | bytes 1572896 | tf_op jit(solution)/shard_map/ppermute | solution.py:22
  46.1 1.2 copy-done.5
  47.2 0.1 slice.12
  47.3 3.5 %collective-permute-start.2 = (f32[2,2,256,256]{3,2,1,0:T(8,128)S(1)}, f32[2,2,256,256]{3,2,1,0:T(8,128)S(1)}, u32[]{:S(2)}, u32[]{:S(2)}) collective-permute-start(f32[2,2,256,256]{3,2,1,0:T(8,128)S(1)} %slice.12), channel_id=1, source_target_pairs={{8,0},{16,8},{24,16},{9,1},{17,9},{25,17},{10,2},{18,10},{26,18},{... | collective-permute-start | bytes 3145736 | tf_op jit(solution)/shard_map/ppermute | solution.py:22
  50.8 0.0 copy-done.6
  50.8 0.1 copy.12
  50.9 0.1 reshape.9
  51.6 0.1 pad_add_fusion.1
  51.7 4.0 %collective-permute-start.3 = (s32[7]{0:T(128)S(1)}, s32[7]{0:T(128)S(1)}, u32[]{:S(2)}, u32[]{:S(2)}) collective-permute-start(s32[7]{0:T(128)S(1)} %pad_add_fusion.1), channel_id=1, source_target_pairs={{0,1},{1,2},{2,3},{3,4},{4,5},{5,6},{6,7},{8,9},{9,10},{10,11},{11... | collective-permute-start | bytes 92 | tf_op jit(solution)/shard_map/ppermute | solution.py:22
  55.7 0.1 pad_add_fusion
  55.8 1.1 collective-permute-done.3
  56.9 0.1 pad_add_fusion.2
  56.9 4.2 %collective-permute-start.4 = (s32[14]{0:T(128)S(1)}, s32[14]{0:T(128)S(1)}, u32[]{:S(2)}, u32[]{:S(2)}) collective-permute-start(s32[14]{0:T(128)S(1)} %pad_add_fusion.2), channel_id=1, source_target_pairs={{0,8},{8,16},{16,24},{1,9},{9,17},{17,25},{2,10},{10,18},{18,26},{... | collective-permute-start | bytes 176 | tf_op jit(solution)/shard_map/ppermute | solution.py:22
  61.1 0.6 broadcast_subtract_fusion.corners
  61.7 0.1 collective-permute-done.4
  61.8 0.1 pad_add_fusion.3
  61.9 0.0 collective-permute-done.1.lower
  61.9 2.5 collective-permute-done.2.corner
  64.4 1.0 copy-done.7
  65.3 58.7 %shard_map.95 = (f32[2,2,384,512]{3,2,1,0:T(8,128)}, f32[2,2,384,256]{3,2,1,0:T(8,128)}, f32[2,2,256,512]{3,2,1,0:T(8,128)}, f32[2,2,256,256]{3,2,1,0:T(8,128)}, f32[6,2,256,256]{3,2,1,0:T(8,128)}) custom-call(s32[3,2]{1,0:T(4,128)} %broadcast_subtract_fusion.corners, s32[1]{0:T(128)S(6)} %copy.15.used, f32[2,2,384,512]{3,2,1,0:T(8,128)} %tile.22, ...), custom_call_target="tpu_custom_call" | custom-call | flops 28999999488 | bytes 30000000 | tf_op jit(solution)/shard_map/pallas_call | solution.py:172
  124.0 1.9 collective-permute-start.7
  126.0 23.9 %collective-permute-start.6 = (f32[2,2,256,512]{3,2,1,0:T(8,128)}, f32[2,2,256,512]{3,2,1,0:T(8,128)}, u32[]{:S(2)}, u32[]{:S(2)}) collective-permute-start(f32[2,2,256,512]{3,2,1,0:T(8,128)} %get-tuple-element.21), channel_id=1, source_target_pairs={{0,8},{8,16},{16,24},{1,9},{9,17},{17,25},{2,10},{10,18},{18,26},{... | collective-permute-start | bytes 6291464 | tf_op jit(solution)/shard_map/ppermute | solution.py:22
  149.9 1.9 collective-permute-start.5
  151.8 0.0 copy-start.1
  151.8 0.0 all-reduce.2.cloned.1.call-update
  151.9 0.0 collective-permute-done.7
  151.9 2.2 collective-permute-start.8
  154.1 0.1 tile.8
  154.1 0.1 pad_add_fusion.4
  154.2 0.1 tile.20
  154.3 1.9 copy-done.2
  156.2 3.7 %shard_map.96.light = f32[384,512]{1,0:T(8,128)S(1)} custom-call(s32[28]{0:T(128)S(1)} %sub.16.info, f32[6,2,256,256]{3,2,1,0:T(8,128)S(1)} %copy-done.2), custom_call_target="tpu_custom_call" | custom-call | flops 10000000 | bytes 12000000 | tf_op jit(solution)/shard_map/pallas_call | solution.py:222
  159.9 44.5 %collective-permute-done.5.left = f32[2,2,384,256]{3,2,1,0:T(8,128)} collective-permute-done((f32[2,2,384,256]{3,2,1,0:T(8,128)}, f32[2,2,384,256]{3,2,1,0:T(8,128)}, u32[]{:S(2)}, u32[]{:S(2)}) %collective-permute-start.5) | collective-permute-done | bytes 1572896 | tf_op jit(solution)/shard_map/ppermute | solution.py:22
  204.4 0.0 collective-permute-done.6.above
  204.4 26.0 %collective-permute-done.8.corner = f32[2,2,256,256]{3,2,1,0:T(8,128)} collective-permute-done((f32[2,2,256,256]{3,2,1,0:T(8,128)}, f32[2,2,256,256]{3,2,1,0:T(8,128)}, u32[]{:S(2)}, u32[]{:S(2)}) %collective-permute-start.8) | collective-permute-done | bytes 1048608 | tf_op jit(solution)/shard_map/ppermute | solution.py:22
  230.4 0.0 copy-done.1
  230.4 4.8 %shard_map.97 = f32[2,2,384,512]{3,2,1,0:T(8,128)} custom-call(f32[2,2,384,512]{3,2,1,0:T(8,128)S(1)} %copy-done.1, f32[2,2,384,512]{3,2,1,0:T(8,128)S(1)} %copy-done.4, f32[2,2,384,256]{3,2,1,0:T(8,128)} %collective-permute-done.5.left, f32[2,2,256,512]{3,2,1,0:T(8,128)} %collective-permute-done.6.above, f32[2,2,256,256]{3,2,1,0:T(8,128)} %collective-permute-done.8.corner, ...), custom_call_target="tpu_custom_call" | custom-call | flops 4000000 | bytes 14000000 | tf_op jit(solution)/shard_map/pallas_call | solution.py:247
  235.2 64.6 %all-reduce.2.cloned.1.call-done = f32[6,2,256,256]{3,2,1,0:T(8,128)} async-done(((f32[6,2,256,256]{3,2,1,0:T(8,128)}), f32[6,2,256,256]{3,2,1,0:T(8,128)}) %all-reduce.2.cloned.1.call-update) | async-done | bytes 3145744 | tf_op jit(solution)/shard_map/psum | solution.py:288
  299.8 3.3 %multiply_reduce_fusion = f32[]{:T(128)} fusion(f32[6,2,256,256]{3,2,1,0:T(8,128)} %all-reduce.2.cloned.1.call-done), kind=kLoop, calls=%fused_computation.1 | loop fusion | flops 1572863 | bytes 3145732 | tf_op jit(solution)/shard_map/reduce_sum | solution.py:295
  303.8 4.0 %divide_subtract_fusion = f32[6,2,256,256]{3,2,1,0:T(8,128)} fusion(f32[6,2,256,256]{3,2,1,0:T(8,128)S(1)} %copy-done.3, f32[6,2,256,256]{3,2,1,0:T(8,128)} %all-reduce.2.cloned.1.call-done, f32[]{:T(128)S(6)} %sqrt.3), kind=kLoop, calls=%fused_computation | loop fusion | flops 2359296 | bytes 9437188 | tf_op jit(solution)/shard_map/sub | solution.py:296
  (10 shorter events, 0.0 us)
Async XLA Ops:
  7.2 4.8 %copy-start = (f32[2,2,384,512]{3,2,1,0:T(8,128)S(1)}, f32[2,2,384,512]{3,2,1,0:T(8,128)}, u32[]{:S(2)}) copy-start(f32[2,2,384,512]{3,2,1,0:T(8,128)} %tile.22) | copy-start | bytes 9437188
  7.2 292.6 %all-reduce.2.cloned.1.call-start = ((), (), s32[]{:S(2)}) async-start(), calls=%async_computation | async-start | bytes 6291456 | tf_op jit(solution)/shard_map/psum | solution.py:288
  8.9 41.9 %copy-start.6 = (s32[3,2]{0,1:T(2,128)S(1)}, s32[3,2]{0,1:T(2,128)}, u32[]{:S(2)}) copy-start(s32[3,2]{0,1:T(2,128)} %param.10) | copy-start | bytes 76
  8.9 37.2 %collective-permute-start = (f32[2,2,384,256]{3,2,1,0:T(8,128)S(1)}, f32[2,2,384,256]{3,2,1,0:T(8,128)S(1)}, u32[]{:S(2)}, u32[]{:S(2)}) collective-permute-start(f32[2,2,384,256]{3,2,1,0:T(8,128)S(1)} %slice.9), channel_id=1, source_target_pairs={{1,0},{2,1},{3,2},{4,3},{5,4},{6,5},{7,6},{9,8},{10,9},{11,10},{12... | collective-permute-start | bytes 4718600 | tf_op jit(solution)/shard_map/ppermute | solution.py:22
  13.4 48.5 %collective-permute-start.1 = (f32[2,2,256,512]{3,2,1,0:T(8,128)}, f32[2,2,256,512]{3,2,1,0:T(8,128)}, u32[]{:S(2)}, u32[]{:S(2)}) collective-permute-start(f32[2,2,256,512]{3,2,1,0:T(8,128)} %slice.10), channel_id=1, source_target_pairs={{8,0},{16,8},{24,16},{9,1},{17,9},{25,17},{10,2},{18,10},{26,18},{... | collective-permute-start | bytes 6291464 | tf_op jit(solution)/shard_map/ppermute | solution.py:22
  46.1 1.2 copy-start.5
  47.3 17.1 %collective-permute-start.2 = (f32[2,2,256,256]{3,2,1,0:T(8,128)S(1)}, f32[2,2,256,256]{3,2,1,0:T(8,128)S(1)}, u32[]{:S(2)}, u32[]{:S(2)}) collective-permute-start(f32[2,2,256,256]{3,2,1,0:T(8,128)S(1)} %slice.12), channel_id=1, source_target_pairs={{8,0},{16,8},{24,16},{9,1},{17,9},{25,17},{10,2},{18,10},{26,18},{... | collective-permute-start | bytes 3145736 | tf_op jit(solution)/shard_map/ppermute | solution.py:22
  51.7 5.2 %collective-permute-start.3 = (s32[7]{0:T(128)S(1)}, s32[7]{0:T(128)S(1)}, u32[]{:S(2)}, u32[]{:S(2)}) collective-permute-start(s32[7]{0:T(128)S(1)} %pad_add_fusion.1), channel_id=1, source_target_pairs={{0,1},{1,2},{2,3},{3,4},{4,5},{5,6},{6,7},{8,9},{9,10},{10,11},{11... | collective-permute-start | bytes 92 | tf_op jit(solution)/shard_map/ppermute | solution.py:22
  56.9 4.9 %collective-permute-start.4 = (s32[14]{0:T(128)S(1)}, s32[14]{0:T(128)S(1)}, u32[]{:S(2)}, u32[]{:S(2)}) collective-permute-start(s32[14]{0:T(128)S(1)} %pad_add_fusion.2), channel_id=1, source_target_pairs={{0,8},{8,16},{16,24},{1,9},{9,17},{17,25},{2,10},{10,18},{18,26},{... | collective-permute-start | bytes 176 | tf_op jit(solution)/shard_map/ppermute | solution.py:22
  64.4 1.0 copy-start.7
  124.0 27.8 %collective-permute-start.7 = (f32[2,2,256,256]{3,2,1,0:T(8,128)}, f32[2,2,256,256]{3,2,1,0:T(8,128)}, u32[]{:S(2)}, u32[]{:S(2)}) collective-permute-start(f32[2,2,256,256]{3,2,1,0:T(8,128)} %get-tuple-element.22), channel_id=1, source_target_pairs={{0,8},{8,16},{16,24},{1,9},{9,17},{17,25},{2,10},{10,18},{18,26},{... | collective-permute-start | bytes 3145736 | tf_op jit(solution)/shard_map/ppermute | solution.py:22
  126.0 78.5 %collective-permute-start.6 = (f32[2,2,256,512]{3,2,1,0:T(8,128)}, f32[2,2,256,512]{3,2,1,0:T(8,128)}, u32[]{:S(2)}, u32[]{:S(2)}) collective-permute-start(f32[2,2,256,512]{3,2,1,0:T(8,128)} %get-tuple-element.21), channel_id=1, source_target_pairs={{0,8},{8,16},{16,24},{1,9},{9,17},{17,25},{2,10},{10,18},{18,26},{... | collective-permute-start | bytes 6291464 | tf_op jit(solution)/shard_map/ppermute | solution.py:22
  149.9 54.5 %collective-permute-start.5 = (f32[2,2,384,256]{3,2,1,0:T(8,128)}, f32[2,2,384,256]{3,2,1,0:T(8,128)}, u32[]{:S(2)}, u32[]{:S(2)}) collective-permute-start(f32[2,2,384,256]{3,2,1,0:T(8,128)} %get-tuple-element.20), channel_id=1, source_target_pairs={{0,1},{1,2},{2,3},{3,4},{4,5},{5,6},{6,7},{8,9},{9,10},{10,11},{11... | collective-permute-start | bytes 4718600 | tf_op jit(solution)/shard_map/ppermute | solution.py:22
  151.8 78.6 %copy-start.1 = (f32[2,2,384,512]{3,2,1,0:T(8,128)S(1)}, f32[2,2,384,512]{3,2,1,0:T(8,128)}, u32[]{:S(2)}) copy-start(f32[2,2,384,512]{3,2,1,0:T(8,128)} %tile.22) | copy-start | bytes 9437188
  151.9 78.5 %collective-permute-start.8 = (f32[2,2,256,256]{3,2,1,0:T(8,128)}, f32[2,2,256,256]{3,2,1,0:T(8,128)}, u32[]{:S(2)}, u32[]{:S(2)}) collective-permute-start(f32[2,2,256,256]{3,2,1,0:T(8,128)} %collective-permute-done.7), channel_id=1, source_target_pairs={{0,1},{1,2},{2,3},{3,4},{4,5},{5,6},{6,7},{8,9},{9,10},{10,11},{11... | collective-permute-start | bytes 3145736 | tf_op jit(solution)/shard_map/ppermute | solution.py:22
  154.3 1.9 copy-start.2
  156.2 74.2 %copy-start.4 = (f32[2,2,384,512]{3,2,1,0:T(8,128)S(1)}, f32[2,2,384,512]{3,2,1,0:T(8,128)}, u32[]{:S(2)}) copy-start(f32[2,2,384,512]{3,2,1,0:T(8,128)} %get-tuple-element.19.grad) | copy-start | bytes 9437188
  235.2 68.6 %copy-start.3 = (f32[6,2,256,256]{3,2,1,0:T(8,128)S(1)}, f32[6,2,256,256]{3,2,1,0:T(8,128)}, u32[]{:S(2)}) copy-start(f32[6,2,256,256]{3,2,1,0:T(8,128)} %probe.3) | copy-start | bytes 9437188
Sparse Core Ops, SparseCore 0:
  152.0 147.7 all-reduce.1
where the time goes:
time: 319 us; the launch traced here: 315 us
  waiting for transfers between devices  168 us (53%)
  Pallas kernels  67.2 us (21%)
  starting transfers between devices  47.5 us (15%)
  between operations  15.6 us (5%)
  other arithmetic  8.25 us (3%)
  local copies, waits for them, and re-layouts  7.64 us (2%)
    ppermute x9, waiting for transfers between devices, from_behind(): return lax.ppermute(array, axis, pairs)  104 us
    psum x1, waiting for transfers between devices, on_device(): summed = lax.psum(grad_probe, ('obj', 'scan'))  64.6 us
    pallas_call x1, Pallas kernels, run_slots(): pl.pallas_call(slots_kernel, out_shape=(jax.ShapeDtypeStruct(tile.shape,...  58.7 us
    ppermute x9, starting transfers between devices, from_behind(): return lax.ppermute(array, axis, pairs)  47.4 us
  transfers between devices with their start and end apart: 10, of which 7 were waited for; matrix products, arithmetic and copies ran while one was open for 1% of the time, Pallas kernels for 3%

commit v1 on v0

--- a/solution.py
+++ b/solution.py
@@ -22,21 +22,29 @@
     return lax.ppermute(array, axis, pairs)
 
 
-def dft_matrix(pattern, sign_factor):
+def dft_parts(pattern):
     indices = np.arange(pattern)
     angles = (indices[:, None] * indices[None, :] % pattern) * (2.0 * math.pi / pattern)
-    real_part = np.cos(angles) / math.sqrt(pattern)
-    imag_part = sign_factor * np.sin(angles) / math.sqrt(pattern)
+    parts = (np.cos(angles) / math.sqrt(pattern), np.sin(angles) / math.sqrt(pattern))
+    return [part.astype(np.float32).astype(jnp.bfloat16).astype(np.float64) for part in parts]
+
+
+def block_matrix(real_part, imag_part):
     upper = np.concatenate([real_part, -imag_part], axis=1)
     lower = np.concatenate([imag_part, real_part], axis=1)
     return jnp.asarray(np.concatenate([upper, lower], axis=0).astype(np.float32), jnp.bfloat16)
 
 
-def propagator(pattern):
+def tables(pattern):
+    cos, sin = dft_parts(pattern)
     indices = np.arange(pattern)
     freqs = ((indices + pattern // 2) % pattern - pattern // 2) / pattern
-    phases = -math.pi * chirp_scale * (freqs[:, None] ** 2 + freqs[None, :] ** 2)
-    return jnp.asarray(np.stack([np.cos(phases), np.sin(phases)], axis=0).astype(np.float32))
+    chirp = np.exp(-1j * math.pi * chirp_scale * freqs**2)
+    hop = (cos + 1j * sin) @ (chirp[:, None] * (cos - 1j * sin))
+    return (
+        block_matrix(cos, -sin), block_matrix(cos, sin),
+        block_matrix(hop.real, hop.imag), block_matrix(hop.real, -hop.imag),
+    )
 
 
 def aligned(row, col):
@@ -64,9 +72,9 @@
 
 
 def slots_kernel(
-    corners, used, tile, right, lower, corner, probe, measured, table_f, table_b, fresnel,
+    corners, used, tile, right, lower, corner, probe, measured, table_f, table_b, hop_f, hop_b,
     grad_tile, grad_right, grad_lower, grad_corner, grad_probe,
-    ext, grad, window, waves, far, intensity, term, sems_in, sems_out,
+    ext, grad, window, waves, far, back, intensity, term, sems_in, sems_out,
 ):
     modes, _, pattern, _ = probe.shape
     layers = tile.shape[0]
@@ -107,32 +115,37 @@
         intensity[...] = jnp.zeros_like(intensity)
         term[...] = jnp.zeros_like(term)
 
-        @pl.loop(0, modes, unroll=2)
-        def _(mode):
-            wr, wi = probe[mode, 0], probe[mode, 1]
-            for layer in range(layers):
+        for layer in range(layers):
+
+            @pl.loop(0, modes, unroll=3)
+            def _(mode, layer=layer):
+                last = layer == layers - 1
+                if layer == 0:
+                    wr, wi = probe[mode, 0], probe[mode, 1]
+                else:
+                    wr, wi = waves[layer - 1, mode, 0], waves[layer - 1, mode, 1]
                 o_r, o_i = window[layer, 0], window[layer, 1]
-                fr, fi = transform(o_r * wr - o_i * wi, o_r * wi + o_i * wr, table_f[...], table_b[...])
-                if layer < layers - 1:
-                    hr, hi = fresnel[0], fresnel[1]
-                    wr, wi = transform(hr * fr - hi * fi, hr * fi + hi * fr, table_b[...], table_f[...])
-                    waves[layer, mode, 0] = wr
-                    waves[layer, mode, 1] = wi
-            far[mode, 0] = fr
-            far[mode, 1] = fi
-            intensity[...] += fr * fr + fi * fi
+                tables = (table_f, table_b) if last else (hop_f, hop_b)
+                fr, fi = transform(o_r * wr - o_i * wi, o_r * wi + o_i * wr, tables[0][...], tables[1][...])
+                if last:
+                    far[mode, 0] = fr
+                    far[mode, 1] = fi
+                    intensity[...] += fr * fr + fi * fi
+                else:
+                    waves[layer, mode, 0] = fr
+                    waves[layer, mode, 1] = fi
 
         intensity[...] = intensity[...] - measured[slot]
 
-        @pl.loop(0, modes, unroll=2)
-        def _(mode):
-            gain = intensity[...]
-            gr, gi = transform(gain * far[mode, 0], gain * far[mode, 1], table_b[...], table_f[...])
-            for layer in reversed(range(layers)):
-                if layer < layers - 1:
-                    sr, si = transform(gr, gi, table_f[...], table_b[...])
-                    hr, hi = fresnel[0], fresnel[1]
-                    gr, gi = transform(hr * sr + hi * si, hr * si - hi * sr, table_b[...], table_f[...])
+        for layer in reversed(range(layers)):
+
+            @pl.loop(0, modes, unroll=3)
+            def _(mode, layer=layer):
+                if layer == layers - 1:
+                    gain = intensity[...]
+                    gr, gi = transform(gain * far[mode, 0], gain * far[mode, 1], table_b[...], table_f[...])
+                else:
+                    gr, gi = transform(back[mode, 0], back[mode, 1], hop_b[...], hop_f[...])
                 if layer == 0:
                     wr, wi = probe[mode, 0], probe[mode, 1]
                 else:
@@ -141,8 +154,12 @@
                 term[layer, 1] += wr * gi - wi * gr
                 o_r, o_i = window[layer, 0], window[layer, 1]
                 gr, gi = o_r * gr + o_i * gi, o_r * gi - o_i * gr
-            grad_probe[mode, 0] += gr
-            grad_probe[mode, 1] += gi
+                if layer == 0:
+                    grad_probe[mode, 0] += gr
+                    grad_probe[mode, 1] += gi
+                else:
+                    back[mode, 0] = gr.astype(jnp.bfloat16)
+                    back[mode, 1] = gi.astype(jnp.bfloat16)
 
         for layer in range(layers):
             for part in range(2):
@@ -161,7 +178,7 @@
         save.wait()
 
 
-def run_slots(corners, used, tile, right, lower, corner, probe, measured, table_f, table_b, fresnel):
+def run_slots(corners, used, tile, right, lower, corner, probe, measured, table_f, table_b, hop_f, hop_b):
     layers, _, height, width = tile.shape
     modes, _, pattern, _ = probe.shape
     smem = pl.BlockSpec(memory_space=pltpu.SMEM)
@@ -178,7 +195,7 @@
             jax.ShapeDtypeStruct(corner.shape, f32),
             jax.ShapeDtypeStruct(probe.shape, f32),
         ),
-        in_specs=[smem, smem, anyw, anyw, anyw, anyw, vmem, vmem, vmem, vmem, vmem],
+        in_specs=[smem, smem, anyw, anyw, anyw, anyw, vmem, vmem, vmem, vmem, vmem, vmem],
         out_specs=(anyw, anyw, anyw, anyw, vmem),
         scratch_shapes=[
             pltpu.VMEM(ext_shape, f32),
@@ -186,6 +203,7 @@
             pltpu.VMEM((layers, 2, pattern, pattern), f32),
             pltpu.VMEM((layers - 1, modes, 2, pattern, pattern), f32),
             pltpu.VMEM((modes, 2, pattern, pattern), f32),
+            pltpu.VMEM((modes, 2, pattern, pattern), jnp.bfloat16),
             pltpu.VMEM((pattern, pattern), f32),
             pltpu.VMEM((layers, 2, pattern, pattern), f32),
             pltpu.SemaphoreType.DMA((4,)),
@@ -193,7 +211,7 @@
         ],
         compiler_params=pltpu.CompilerParams(vmem_limit_bytes=vmem_bytes),
         cost_estimate=pl.CostEstimate(flops=29_000_000_000, bytes_accessed=30_000_000, transcendentals=0),
-    )(corners, used, tile, right, lower, corner, probe, measured, table_f, table_b, fresnel)
+    )(corners, used, tile, right, lower, corner, probe, measured, table_f, table_b, hop_f, hop_b)
 
 
 def light_kernel(height, width, slots, info, probe, light, canvas, power):
@@ -263,9 +281,7 @@
     tile_width = object_slab.shape[3]
     pattern = probe_mode_stack.shape[-1]
     slots = offsets.shape[0]
-    table_f = dft_matrix(pattern, -1.0)
-    table_b = dft_matrix(pattern, 1.0)
-    fresnel = propagator(pattern)
+    table_f, table_b, hop_f, hop_b = tables(pattern)
     right_rim = from_behind(object_slab[:, :, :, :pattern], "scan", -1)
     lower_rim = from_behind(object_slab[:, :, :pattern, :], "obj", -1)
     corner_rim = from_behind(right_rim[:, :, :pattern, :], "obj", -1)
@@ -283,7 +299,7 @@
     light = run_light(tile_height, tile_width, slots, info - shifts, probe_mode_stack)
     grad_tile, grad_right, grad_lower, grad_corner, grad_probe = run_slots(
         corners, counts, object_slab, right_rim, lower_rim, corner_rim, probe_mode_stack,
-        measured, table_f, table_b, fresnel,
+        measured, table_f, table_b, hop_f, hop_b,
     )
     summed = lax.psum(grad_probe, ("obj", "scan"))
     corner_half = from_behind(grad_corner, "obj", 1)

time: 319 us -> 287 us (0.90)
  Pallas kernels: 67.2 us -> 31.6 us
  starting transfers between devices: 47.5 us -> 63 us
  waiting for transfers between devices: 168 us -> 156 us
    pallas_call x1, Pallas kernels: 58.7 us -> 23.8 us  [run_slots(): pl.pallas_call(slots_kernel, out_shape=(jax.ShapeDtypeStruct(tile.shape,...]
    ppermute x9, waiting for transfers between devices: 104 us -> 81.2 us  [from_behind(): return lax.ppermute(array, axis, pairs)]
    ppermute x9, starting transfers between devices: 47.4 us -> 62.9 us  [from_behind(): return lax.ppermute(array, axis, pairs)]
    psum x1, waiting for transfers between devices: 64.6 us -> 74.7 us  [on_device(): summed = lax.psum(grad_probe, ('obj', 'scan'))]
where the time goes in v1:
time: 287 us; the launch traced here: 282 us
  waiting for transfers between devices  156 us (54%)
  starting transfers between devices  63 us (22%)
  Pallas kernels  31.6 us (11%)
  between operations  15.6 us (5%)
  other arithmetic  8.25 us (3%)
  local copies, waits for them, and re-layouts  7.68 us (3%)
    ppermute x9, waiting for transfers between devices, from_behind(): return lax.ppermute(array, axis, pairs)  81.2 us
    psum x1, waiting for transfers between devices, on_device(): summed = lax.psum(grad_probe, ('obj', 'scan'))  74.7 us
    ppermute x9, starting transfers between devices, from_behind(): return lax.ppermute(array, axis, pairs)  62.9 us
    pallas_call x1, Pallas kernels, run_slots(): pl.pallas_call(slots_kernel, out_shape=(jax.ShapeDtypeStruct(tile.shape,...  23.8 us
  transfers between devices with their start and end apart: 10, of which 7 were waited for; matrix products, arithmetic and copies ran while one was open for 1% of the time, Pallas kernels for 3%

profile of v1, /device:TPU:17, one launch (start us, length us, event | category | flops | bytes accessed | tf_op | source)
XLA Modules:
  0.0 281.9 jit_solution(6719220505140296298)
XLA Ops:
  7.2 0.0 copy-start
  7.2 0.0 all-reduce.2.cloned.1.call-start
  7.2 1.7 slice.9
  8.9 0.0 copy-start.6
  8.9 3.0 %collective-permute-start = (f32[2,2,384,256]{3,2,1,0:T(8,128)S(1)}, f32[2,2,384,256]{3,2,1,0:T(8,128)S(1)}, u32[]{:S(2)}, u32[]{:S(2)}) collective-permute-start(f32[2,2,384,256]{3,2,1,0:T(8,128)S(1)} %slice.9), channel_id=1, source_target_pairs={{1,0},{2,1},{3,2},{4,3},{5,4},{6,5},{7,6},{9,8},{10,9},{11,10},{12... | collective-permute-start | bytes 4718600 | tf_op jit(solution)/shard_map/ppermute | solution.py:22
  11.9 0.0 copy-done
  11.9 1.5 slice.10
  13.4 2.9 %collective-permute-start.1 = (f32[2,2,256,512]{3,2,1,0:T(8,128)}, f32[2,2,256,512]{3,2,1,0:T(8,128)}, u32[]{:S(2)}, u32[]{:S(2)}) collective-permute-start(f32[2,2,256,512]{3,2,1,0:T(8,128)} %slice.10), channel_id=1, source_target_pairs={{8,0},{16,8},{24,16},{9,1},{17,9},{25,17},{10,2},{18,10},{26,18},{... | collective-permute-start | bytes 6291464 | tf_op jit(solution)/shard_map/ppermute | solution.py:22
  16.3 29.8 %collective-permute-done.right = f32[2,2,384,256]{3,2,1,0:T(8,128)S(1)} collective-permute-done((f32[2,2,384,256]{3,2,1,0:T(8,128)S(1)}, f32[2,2,384,256]{3,2,1,0:T(8,128)S(1)}, u32[]{:S(2)}, u32[]{:S(2)}) %collective-permute-start) | collective-permute-done | bytes 1572896 | tf_op jit(solution)/shard_map/ppermute | solution.py:22
  46.1 1.2 copy-done.5
  47.2 0.1 slice.12
  47.3 3.5 %collective-permute-start.2 = (f32[2,2,256,256]{3,2,1,0:T(8,128)S(1)}, f32[2,2,256,256]{3,2,1,0:T(8,128)S(1)}, u32[]{:S(2)}, u32[]{:S(2)}) collective-permute-start(f32[2,2,256,256]{3,2,1,0:T(8,128)S(1)} %slice.12), channel_id=1, source_target_pairs={{8,0},{16,8},{24,16},{9,1},{17,9},{25,17},{10,2},{18,10},{26,18},{... | collective-permute-start | bytes 3145736 | tf_op jit(solution)/shard_map/ppermute | solution.py:22
  50.8 0.1 copy.13
  50.9 0.1 reshape.9
  51.6 0.1 pad_add_fusion.1
  51.7 4.0 %collective-permute-start.3 = (s32[7]{0:T(128)S(1)}, s32[7]{0:T(128)S(1)}, u32[]{:S(2)}, u32[]{:S(2)}) collective-permute-start(s32[7]{0:T(128)S(1)} %pad_add_fusion.1), channel_id=1, source_target_pairs={{0,1},{1,2},{2,3},{3,4},{4,5},{5,6},{6,7},{8,9},{9,10},{10,11},{11... | collective-permute-start | bytes 92 | tf_op jit(solution)/shard_map/ppermute | solution.py:22
  55.7 0.1 pad_add_fusion
  55.8 1.1 collective-permute-done.3
  56.9 0.1 pad_add_fusion.2
  56.9 4.2 %collective-permute-start.4 = (s32[14]{0:T(128)S(1)}, s32[14]{0:T(128)S(1)}, u32[]{:S(2)}, u32[]{:S(2)}) collective-permute-start(s32[14]{0:T(128)S(1)} %pad_add_fusion.2), channel_id=1, source_target_pairs={{0,8},{8,16},{16,24},{1,9},{9,17},{17,25},{2,10},{10,18},{18,26},{... | collective-permute-start | bytes 176 | tf_op jit(solution)/shard_map/ppermute | solution.py:22
  61.1 0.6 broadcast_subtract_fusion.corners
  61.7 0.1 collective-permute-done.4
  61.8 0.1 pad_add_fusion.3
  61.9 0.0 collective-permute-done.1.lower
  61.9 2.5 collective-permute-done.2.corner
  64.4 1.0 copy-done.7
  65.3 23.8 %shard_map.104 = (f32[2,2,384,512]{3,2,1,0:T(8,128)}, f32[2,2,384,256]{3,2,1,0:T(8,128)}, f32[2,2,256,512]{3,2,1,0:T(8,128)}, f32[2,2,256,256]{3,2,1,0:T(8,128)}, f32[6,2,256,256]{3,2,1,0:T(8,128)}) custom-call(s32[3,2]{1,0:T(4,128)} %broadcast_subtract_fusion.corners, s32[1]{0:T(128)S(6)} %copy.16.used, f32[2,2,384,512]{3,2,1,0:T(8,128)} %tile.22, ...), custom_call_target="tpu_custom_call" | custom-call | flops 28999999488 | bytes 30000000 | tf_op jit(solution)/shard_map/pallas_call | solution.py:189
  89.1 1.9 collective-permute-start.7
  91.0 25.7 %collective-permute-start.6 = (f32[2,2,256,512]{3,2,1,0:T(8,128)}, f32[2,2,256,512]{3,2,1,0:T(8,128)}, u32[]{:S(2)}, u32[]{:S(2)}) collective-permute-start(f32[2,2,256,512]{3,2,1,0:T(8,128)} %get-tuple-element.21), channel_id=1, source_target_pairs={{0,8},{8,16},{16,24},{1,9},{9,17},{17,25},{2,10},{10,18},{18,26},{... | collective-permute-start | bytes 6291464 | tf_op jit(solution)/shard_map/ppermute | solution.py:22
  116.7 6.1 %collective-permute-start.5 = (f32[2,2,384,256]{3,2,1,0:T(8,128)}, f32[2,2,384,256]{3,2,1,0:T(8,128)}, u32[]{:S(2)}, u32[]{:S(2)}) collective-permute-start(f32[2,2,384,256]{3,2,1,0:T(8,128)} %get-tuple-element.20), channel_id=1, source_target_pairs={{0,1},{1,2},{2,3},{3,4},{4,5},{5,6},{6,7},{8,9},{9,10},{10,11},{11... | collective-permute-start | bytes 4718600 | tf_op jit(solution)/shard_map/ppermute | solution.py:22
  122.9 0.0 copy-start.1
  122.9 0.0 all-reduce.2.cloned.1.call-update
  122.9 0.0 collective-permute-done.7
  122.9 11.7 %collective-permute-start.8 = (f32[2,2,256,256]{3,2,1,0:T(8,128)}, f32[2,2,256,256]{3,2,1,0:T(8,128)}, u32[]{:S(2)}, u32[]{:S(2)}) collective-permute-start(f32[2,2,256,256]{3,2,1,0:T(8,128)} %collective-permute-done.7), channel_id=1, source_target_pairs={{0,1},{1,2},{2,3},{3,4},{4,5},{5,6},{6,7},{8,9},{9,10},{10,11},{11... | collective-permute-start | bytes 3145736 | tf_op jit(solution)/shard_map/ppermute | solution.py:22
  134.6 0.1 tile.8
  134.7 0.1 pad_add_fusion.4
  134.8 0.1 tile.20
  134.9 1.9 copy-done.2
  136.8 3.0 %shard_map.105.light = f32[384,512]{1,0:T(8,128)S(1)} custom-call(s32[28]{0:T(128)S(1)} %sub.16.info, f32[6,2,256,256]{3,2,1,0:T(8,128)S(1)} %copy-done.2), custom_call_target="tpu_custom_call" | custom-call | flops 10000000 | bytes 12000000 | tf_op jit(solution)/shard_map/pallas_call | solution.py:240
  139.8 32.5 %collective-permute-done.5.left = f32[2,2,384,256]{3,2,1,0:T(8,128)} collective-permute-done((f32[2,2,384,256]{3,2,1,0:T(8,128)}, f32[2,2,384,256]{3,2,1,0:T(8,128)}, u32[]{:S(2)}, u32[]{:S(2)}) %collective-permute-start.5) | collective-permute-done | bytes 1572896 | tf_op jit(solution)/shard_map/ppermute | solution.py:22
  172.3 0.0 collective-permute-done.6.above
  172.3 15.3 %collective-permute-done.8.corner = f32[2,2,256,256]{3,2,1,0:T(8,128)} collective-permute-done((f32[2,2,256,256]{3,2,1,0:T(8,128)}, f32[2,2,256,256]{3,2,1,0:T(8,128)}, u32[]{:S(2)}, u32[]{:S(2)}) %collective-permute-start.8) | collective-permute-done | bytes 1048608 | tf_op jit(solution)/shard_map/ppermute | solution.py:22
  187.6 0.0 copy-done.1
  187.6 4.8 %shard_map.106 = f32[2,2,384,512]{3,2,1,0:T(8,128)} custom-call(f32[2,2,384,512]{3,2,1,0:T(8,128)S(1)} %copy-done.1, f32[2,2,384,512]{3,2,1,0:T(8,128)S(1)} %copy-done.4, f32[2,2,384,256]{3,2,1,0:T(8,128)} %collective-permute-done.5.left, f32[2,2,256,512]{3,2,1,0:T(8,128)} %collective-permute-done.6.above, f32[2,2,256,256]{3,2,1,0:T(8,128)} %collective-permute-done.8.corner, ...), custom_call_target="tpu_custom_call" | custom-call | flops 4000000 | bytes 14000000 | tf_op jit(solution)/shard_map/pallas_call | solution.py:265
  192.4 74.7 %all-reduce.2.cloned.1.call-done = f32[6,2,256,256]{3,2,1,0:T(8,128)} async-done(((f32[6,2,256,256]{3,2,1,0:T(8,128)}), f32[6,2,256,256]{3,2,1,0:T(8,128)}) %all-reduce.2.cloned.1.call-update) | async-done | bytes 3145744 | tf_op jit(solution)/shard_map/psum | solution.py:304
  267.1 3.3 %multiply_reduce_fusion = f32[]{:T(128)} fusion(f32[6,2,256,256]{3,2,1,0:T(8,128)} %all-reduce.2.cloned.1.call-done), kind=kLoop, calls=%fused_computation.1 | loop fusion | flops 1572863 | bytes 3145732 | tf_op jit(solution)/shard_map/reduce_sum | solution.py:311
  271.1 0.0 copy-done.3
  271.1 4.0 %divide_subtract_fusion = f32[6,2,256,256]{3,2,1,0:T(8,128)} fusion(f32[6,2,256,256]{3,2,1,0:T(8,128)S(1)} %copy-done.3, f32[6,2,256,256]{3,2,1,0:T(8,128)} %all-reduce.2.cloned.1.call-done, f32[]{:T(128)S(6)} %sqrt.3), kind=kLoop, calls=%fused_computation | loop fusion | flops 2359296 | bytes 9437188 | tf_op jit(solution)/shard_map/sub | solution.py:312
  (10 shorter events, 0.0 us)
Async XLA Ops:
  7.2 4.8 %copy-start = (f32[2,2,384,512]{3,2,1,0:T(8,128)S(1)}, f32[2,2,384,512]{3,2,1,0:T(8,128)}, u32[]{:S(2)}) copy-start(f32[2,2,384,512]{3,2,1,0:T(8,128)} %tile.22) | copy-start | bytes 9437188
  7.2 259.9 %all-reduce.2.cloned.1.call-start = ((), (), s32[]{:S(2)}) async-start(), calls=%async_computation | async-start | bytes 6291456 | tf_op jit(solution)/shard_map/psum | solution.py:304
  8.9 41.9 %copy-start.6 = (s32[3,2]{0,1:T(2,128)S(1)}, s32[3,2]{0,1:T(2,128)}, u32[]{:S(2)}) copy-start(s32[3,2]{0,1:T(2,128)} %param.11) | copy-start | bytes 76
  8.9 37.2 %collective-permute-start = (f32[2,2,384,256]{3,2,1,0:T(8,128)S(1)}, f32[2,2,384,256]{3,2,1,0:T(8,128)S(1)}, u32[]{:S(2)}, u32[]{:S(2)}) collective-permute-start(f32[2,2,384,256]{3,2,1,0:T(8,128)S(1)} %slice.9), channel_id=1, source_target_pairs={{1,0},{2,1},{3,2},{4,3},{5,4},{6,5},{7,6},{9,8},{10,9},{11,10},{12... | collective-permute-start | bytes 4718600 | tf_op jit(solution)/shard_map/ppermute | solution.py:22
  13.4 48.5 %collective-permute-start.1 = (f32[2,2,256,512]{3,2,1,0:T(8,128)}, f32[2,2,256,512]{3,2,1,0:T(8,128)}, u32[]{:S(2)}, u32[]{:S(2)}) collective-permute-start(f32[2,2,256,512]{3,2,1,0:T(8,128)} %slice.10), channel_id=1, source_target_pairs={{8,0},{16,8},{24,16},{9,1},{17,9},{25,17},{10,2},{18,10},{26,18},{... | collective-permute-start | bytes 6291464 | tf_op jit(solution)/shard_map/ppermute | solution.py:22
  46.1 1.2 copy-start.5
  47.3 17.1 %collective-permute-start.2 = (f32[2,2,256,256]{3,2,1,0:T(8,128)S(1)}, f32[2,2,256,256]{3,2,1,0:T(8,128)S(1)}, u32[]{:S(2)}, u32[]{:S(2)}) collective-permute-start(f32[2,2,256,256]{3,2,1,0:T(8,128)S(1)} %slice.12), channel_id=1, source_target_pairs={{8,0},{16,8},{24,16},{9,1},{17,9},{25,17},{10,2},{18,10},{26,18},{... | collective-permute-start | bytes 3145736 | tf_op jit(solution)/shard_map/ppermute | solution.py:22
  51.7 5.2 %collective-permute-start.3 = (s32[7]{0:T(128)S(1)}, s32[7]{0:T(128)S(1)}, u32[]{:S(2)}, u32[]{:S(2)}) collective-permute-start(s32[7]{0:T(128)S(1)} %pad_add_fusion.1), channel_id=1, source_target_pairs={{0,1},{1,2},{2,3},{3,4},{4,5},{5,6},{6,7},{8,9},{9,10},{10,11},{11... | collective-permute-start | bytes 92 | tf_op jit(solution)/shard_map/ppermute | solution.py:22
  56.9 4.9 %collective-permute-start.4 = (s32[14]{0:T(128)S(1)}, s32[14]{0:T(128)S(1)}, u32[]{:S(2)}, u32[]{:S(2)}) collective-permute-start(s32[14]{0:T(128)S(1)} %pad_add_fusion.2), channel_id=1, source_target_pairs={{0,8},{8,16},{16,24},{1,9},{9,17},{17,25},{2,10},{10,18},{18,26},{... | collective-permute-start | bytes 176 | tf_op jit(solution)/shard_map/ppermute | solution.py:22
  64.4 1.0 copy-start.7
  89.1 33.8 %collective-permute-start.7 = (f32[2,2,256,256]{3,2,1,0:T(8,128)}, f32[2,2,256,256]{3,2,1,0:T(8,128)}, u32[]{:S(2)}, u32[]{:S(2)}) collective-permute-start(f32[2,2,256,256]{3,2,1,0:T(8,128)} %get-tuple-element.22), channel_id=1, source_target_pairs={{0,8},{8,16},{16,24},{1,9},{9,17},{17,25},{2,10},{10,18},{18,26},{... | collective-permute-start | bytes 3145736 | tf_op jit(solution)/shard_map/ppermute | solution.py:22
  91.0 81.2 %collective-permute-start.6 = (f32[2,2,256,512]{3,2,1,0:T(8,128)}, f32[2,2,256,512]{3,2,1,0:T(8,128)}, u32[]{:S(2)}, u32[]{:S(2)}) collective-permute-start(f32[2,2,256,512]{3,2,1,0:T(8,128)} %get-tuple-element.21), channel_id=1, source_target_pairs={{0,8},{8,16},{16,24},{1,9},{9,17},{17,25},{2,10},{10,18},{18,26},{... | collective-permute-start | bytes 6291464 | tf_op jit(solution)/shard_map/ppermute | solution.py:22
  116.7 55.5 %collective-permute-start.5 = (f32[2,2,384,256]{3,2,1,0:T(8,128)}, f32[2,2,384,256]{3,2,1,0:T(8,128)}, u32[]{:S(2)}, u32[]{:S(2)}) collective-permute-start(f32[2,2,384,256]{3,2,1,0:T(8,128)} %get-tuple-element.20), channel_id=1, source_target_pairs={{0,1},{1,2},{2,3},{3,4},{4,5},{5,6},{6,7},{8,9},{9,10},{10,11},{11... | collective-permute-start | bytes 4718600 | tf_op jit(solution)/shard_map/ppermute | solution.py:22
  122.9 64.7 %copy-start.1 = (f32[2,2,384,512]{3,2,1,0:T(8,128)S(1)}, f32[2,2,384,512]{3,2,1,0:T(8,128)}, u32[]{:S(2)}) copy-start(f32[2,2,384,512]{3,2,1,0:T(8,128)} %tile.22) | copy-start | bytes 9437188
  122.9 64.6 %collective-permute-start.8 = (f32[2,2,256,256]{3,2,1,0:T(8,128)}, f32[2,2,256,256]{3,2,1,0:T(8,128)}, u32[]{:S(2)}, u32[]{:S(2)}) collective-permute-start(f32[2,2,256,256]{3,2,1,0:T(8,128)} %collective-permute-done.7), channel_id=1, source_target_pairs={{0,1},{1,2},{2,3},{3,4},{4,5},{5,6},{6,7},{8,9},{9,10},{10,11},{11... | collective-permute-start | bytes 3145736 | tf_op jit(solution)/shard_map/ppermute | solution.py:22
  134.9 1.9 copy-start.2
  136.8 50.8 %copy-start.4 = (f32[2,2,384,512]{3,2,1,0:T(8,128)S(1)}, f32[2,2,384,512]{3,2,1,0:T(8,128)}, u32[]{:S(2)}) copy-start(f32[2,2,384,512]{3,2,1,0:T(8,128)} %get-tuple-element.19.grad) | copy-start | bytes 9437188
  192.4 78.7 %copy-start.3 = (f32[6,2,256,256]{3,2,1,0:T(8,128)S(1)}, f32[6,2,256,256]{3,2,1,0:T(8,128)}, u32[]{:S(2)}) copy-start(f32[6,2,256,256]{3,2,1,0:T(8,128)} %probe.3) | copy-start | bytes 9437188
Sparse Core Ops, SparseCore 0:
  123.0 143.9 all-reduce.1

commit v2 on v1

--- a/solution.py
+++ b/solution.py
@@ -214,6 +214,407 @@
     )(corners, used, tile, right, lower, corner, probe, measured, table_f, table_b, hop_f, hop_b)
 
 
+MESH = pl.DeviceIdType.MESH
+
+
+def place():
+    return lax.axis_index("obj"), lax.axis_index("scan")
+
+
+def greet(partners):
+    barrier = pltpu.get_barrier_semaphore()
+    for exists, device in partners:
+
+        @pl.when(exists)
+        def _(device=device):
+            pl.semaphore_signal(barrier, inc=1, device_id=device, device_id_type=MESH)
+
+    count = 0
+    for exists, _ in partners:
+        count = count + (1 if exists is True else jnp.where(exists, 1, 0))
+    pl.semaphore_wait(barrier, count)
+
+
+def neighbours(rows, cols):
+    row, col = place()
+    return {
+        "up": (row > 0, (row - 1, col)),
+        "down": (row < rows - 1, (row + 1, col)),
+        "left": (col > 0, (row, col - 1)),
+        "right": (col < cols - 1, (row, col + 1)),
+    }
+
+
+def rims_kernel(rows, cols, tile, right, lower, corner, sent, got):
+    near = neighbours(rows, cols)
+    greet(list(near.values()))
+    layers, pattern = tile.shape[0], corner.shape[-1]
+    height = tile.shape[2]
+    has_up, up = near["up"]
+    has_down, _ = near["down"]
+    has_left, left = near["left"]
+    has_right, _ = near["right"]
+
+    def copy(source, target, k, device):
+        return pltpu.make_async_remote_copy(
+            src_ref=source, dst_ref=target, send_sem=sent.at[k], recv_sem=got.at[k],
+            device_id=device, device_id_type=MESH,
+        )
+
+    top, rest = pl.ds(0, pattern), pl.ds(pattern, height - pattern)
+    first = pl.ds(0, pattern)
+    tops = [copy(tile.at[n, :, top, first], right.at[n, :, top], 4 * n, left) for n in range(layers)]
+    rests = [copy(tile.at[n, :, rest, first], right.at[n, :, rest], 4 * n + 1, left) for n in range(layers)]
+    lowers = [copy(tile.at[n, :, top], lower.at[n], 4 * n + 2, up) for n in range(layers)]
+    corners = [copy(right.at[n, :, top], corner.at[n], 4 * n + 3, up) for n in range(layers)]
+    for n in range(layers):
+
+        @pl.when(has_left)
+        def _(n=n):
+            tops[n].start()
+
+        @pl.when(has_up)
+        def _(n=n):
+            lowers[n].start()
+
+        @pl.when(has_left)
+        def _(n=n):
+            rests[n].start()
+
+    for n in range(layers):
+
+        @pl.when(has_right)
+        def _(n=n):
+            tops[n].wait_recv()
+
+            @pl.when(has_up)
+            def _():
+                corners[n].start()
+
+    for n in range(layers):
+
+        @pl.when(has_right)
+        def _(n=n):
+            rests[n].wait_recv()
+
+            @pl.when(has_down)
+            def _():
+                corners[n].wait_recv()
+
+            @pl.when(has_up)
+            def _():
+                corners[n].wait_send()
+
+        @pl.when(has_down)
+        def _(n=n):
+            lowers[n].wait_recv()
+
+        @pl.when(has_left)
+        def _(n=n):
+            tops[n].wait_send()
+            rests[n].wait_send()
+
+        @pl.when(has_up)
+        def _(n=n):
+            lowers[n].wait_send()
+
+
+def run_rims(rows, cols, tile, pattern):
+    layers, _, height, width = tile.shape
+    anyw = pl.BlockSpec(memory_space=pl.ANY)
+    f32 = jnp.float32
+    return pl.pallas_call(
+        functools.partial(rims_kernel, rows, cols),
+        out_shape=(
+            jax.ShapeDtypeStruct((layers, 2, height, pattern), f32),
+            jax.ShapeDtypeStruct((layers, 2, pattern, width), f32),
+            jax.ShapeDtypeStruct((layers, 2, pattern, pattern), f32),
+        ),
+        in_specs=[anyw],
+        out_specs=(anyw,) * 3,
+        scratch_shapes=[pltpu.SemaphoreType.DMA((4 * layers,)), pltpu.SemaphoreType.DMA((4 * layers,))],
+        compiler_params=pltpu.CompilerParams(collective_id=0, has_side_effects=True),
+        cost_estimate=pl.CostEstimate(flops=0, bytes_accessed=10_000_000, transcendentals=0),
+    )(tile)
+
+
+def digits(rows, cols):
+    return {
+        "core": ("obj", 1, 2),
+        "y": ("obj", 2, rows // 2),
+        "x": ("scan", 1, 2),
+        "z": ("scan", 2, cols // 2),
+    }
+
+
+def member(digit, by):
+    axis, stride, radix = digit
+    row, col = place()
+    at = row if axis == "obj" else col
+    mine = at // stride % radix
+    theirs = (mine + by) % radix
+    there = at + (theirs - mine) * stride
+    return mine, theirs, ((there, col) if axis == "obj" else (row, there))
+
+
+def group(digit):
+    return [(True, member(digit, by)[2]) for by in range(1, digit[2])]
+
+
+streams = (
+    (0, 0, 2, ("x", "y", "z")),
+    (1, 0, 2, ("y", "x", "z")),
+    (2, 0, 1, ("x", "z", "y")),
+    (2, 1, 1, ("y", "z", "x")),
+)
+
+
+class Reduction:
+    def __init__(self, rows, cols, grad, total, held, landed, core_in, sems):
+        self.ways = digits(rows, cols)
+        self.grad, self.total, self.held, self.landed, self.core_in = grad, total, held, landed, core_in
+        self.sent, self.got = sems
+        self.count = 0
+        self.pending = []
+        self.share = grad.shape[0] // 2
+        self.state = [[0, grad.shape[1]] for _ in streams]
+        self.waits = [[] for _ in streams]
+        self.landing = [0 for _ in streams]
+
+    def copy(self, source, target, device):
+        k = self.count
+        self.count += 1
+        made = pltpu.make_async_remote_copy(
+            src_ref=source, dst_ref=target, send_sem=self.sent.at[k], recv_sem=self.got.at[k],
+            device_id=device, device_id_type=MESH,
+        )
+        made.start()
+        self.pending.append(made)
+        return made
+
+    def core_send(self, k):
+        mine, theirs, device = member(self.ways["core"], 1)
+        self.core_waits = getattr(self, "core_waits", {})
+        self.core_waits[k] = self.copy(self.grad.at[theirs * self.share + k], self.core_in.at[k], device)
+
+    def core_add(self, k):
+        mine, _, _ = member(self.ways["core"], 1)
+        self.core_waits[k].wait_recv()
+        self.held[k] = self.grad[mine * self.share + k] + self.core_in[k]
+
+    def lanes_of(self, s):
+        return pl.ds(streams[s][1] * lanes, streams[s][2] * lanes)
+
+    def scatter_send(self, s, step):
+        mode = streams[s][0]
+        digit = self.ways[streams[s][3][step]]
+        start, size = self.state[s]
+        part = size // digit[2]
+        self.waits[s] = []
+        for by in range(1, digit[2]):
+            _, theirs, device = member(digit, by)
+            spot = self.landed.at[mode, pl.ds(self.landing[s], part), self.lanes_of(s)]
+            source = self.held.at[mode, pl.ds(pl.multiple_of(start + theirs * part, sublanes), part), self.lanes_of(s)]
+            self.waits[s].append((self.copy(source, spot, device), self.landing[s]))
+            self.landing[s] += part
+
+    def scatter_add(self, s, step):
+        mode = streams[s][0]
+        digit = self.ways[streams[s][3][step]]
+        start, size = self.state[s]
+        part = size // digit[2]
+        if digit[2] > 1:
+            mine, _, _ = member(digit, 1)
+            start = start + mine * part
+        self.state[s] = [start, part]
+        span = pl.ds(pl.multiple_of(start, sublanes), part)
+        value = self.held[mode, span, self.lanes_of(s)]
+        for made, landing in self.waits[s]:
+            made.wait_recv()
+            value = value + self.landed[mode, pl.ds(landing, part), self.lanes_of(s)]
+        if step == 2:
+            own = member(self.ways["core"], 1)[0] * self.share + mode
+            self.total[own, span, self.lanes_of(s)] = value
+        else:
+            self.held[mode, span, self.lanes_of(s)] = value
+
+    def gather_send(self, s, step):
+        mode = streams[s][0]
+        digit = self.ways[streams[s][3][step]]
+        start, size = self.state[s]
+        own = member(self.ways["core"], 1)[0] * self.share + mode
+        self.waits[s] = []
+        for by in range(1, digit[2]):
+            spot = self.total.at[own, pl.ds(pl.multiple_of(start, sublanes), size), self.lanes_of(s)]
+            self.waits[s].append(self.copy(spot, spot, member(digit, by)[2]))
+
+    def gather_wait(self, s, step):
+        digit = self.ways[streams[s][3][step]]
+        start, size = self.state[s]
+        for made in self.waits[s]:
+            made.wait_recv()
+        if digit[2] > 1:
+            start = start - member(digit, 1)[0] * size
+        self.state[s] = [start, size * digit[2]]
+
+    def core_share(self, s):
+        mine, _, device = member(self.ways["core"], 1)
+        spot = self.total.at[mine * self.share + streams[s][0], :, self.lanes_of(s)]
+        self.waits[s] = [self.copy(spot, spot, device)]
+
+    def run(self):
+        every = range(len(streams))
+        for k in range(self.share):
+            self.core_add(k)
+            for s in every:
+                if streams[s][0] == k:
+                    self.scatter_send(s, 0)
+        for step in range(3):
+            for s in every:
+                self.scatter_add(s, step)
+                if step < 2:
+                    self.scatter_send(s, step + 1)
+                else:
+                    self.gather_send(s, 2)
+        for step in (2, 1, 0):
+            for s in every:
+                self.gather_wait(s, step)
+                if step:
+                    self.gather_send(s, step - 1)
+                else:
+                    self.core_share(s)
+        for s in every:
+            for made in self.waits[s]:
+                made.wait_recv()
+        for made in self.pending:
+            made.wait_send()
+
+
+def share_kernel(
+    rows, cols, right, lower, corner, grad, from_left, from_above, total,
+    side, edge, held, landed, core_in, sems_in, sent, got, sent_halo, got_halo,
+):
+    near = neighbours(rows, cols)
+    ways = digits(rows, cols)
+    partners = list(near.values())
+    for digit in ways.values():
+        partners += group(digit)
+    layers, pattern = right.shape[0], corner.shape[-1]
+    height = right.shape[2]
+    loads = [
+        pltpu.make_async_copy(right, side, sems_in.at[0]),
+    ]
+    for load in loads:
+        load.start()
+    greet(partners)
+    has_up, up = near["up"]
+    has_down, down = near["down"]
+    has_left, _ = near["left"]
+    has_right, far_right = near["right"]
+
+    def copy(source, target, k, device):
+        return pltpu.make_async_remote_copy(
+            src_ref=source, dst_ref=target, send_sem=sent_halo.at[k], recv_sem=got_halo.at[k],
+            device_id=device, device_id_type=MESH,
+        )
+
+    top, rest = pl.ds(0, pattern), pl.ds(pattern, height - pattern)
+    tops = [copy(side.at[n, :, top], from_left.at[n, :, top], 4 * n, far_right) for n in range(layers)]
+    rests = [copy(side.at[n, :, rest], from_left.at[n, :, rest], 4 * n + 1, far_right) for n in range(layers)]
+    lowers = [copy(lower.at[n], from_above.at[n], 4 * n + 2, down) for n in range(layers)]
+    corners = [copy(corner.at[n], edge.at[n], 4 * n + 3, down) for n in range(layers)]
+    reduction = Reduction(rows, cols, grad, total, held, landed, core_in, (sent, got))
+    for k in range(reduction.share):
+        reduction.core_send(k)
+
+    @pl.when(has_down)
+    def _():
+        @pl.when(has_right)
+        def _():
+            for n in range(layers):
+                corners[n].start()
+
+        for n in range(layers):
+            lowers[n].start()
+
+    for load in loads:
+        load.wait()
+
+    @pl.when(has_right)
+    def _():
+        for n in range(layers):
+            rests[n].start()
+        for n in range(layers):
+
+            @pl.when(has_up)
+            def _(n=n):
+                corners[n].wait_recv()
+                side[n, :, :pattern] = side[n, :, :pattern] + edge[n]
+
+            tops[n].start()
+
+    reduction.run()
+
+    @pl.when(has_right)
+    def _():
+        for n in range(layers):
+            rests[n].wait_send()
+            tops[n].wait_send()
+
+            @pl.when(has_down)
+            def _(n=n):
+                corners[n].wait_send()
+
+    @pl.when(has_down)
+    def _():
+        for n in range(layers):
+            lowers[n].wait_send()
+
+    @pl.when(has_left)
+    def _():
+        for n in range(layers):
+            rests[n].wait_recv()
+            tops[n].wait_recv()
+
+    @pl.when(has_up)
+    def _():
+        for n in range(layers):
+            lowers[n].wait_recv()
+
+
+def run_share(rows, cols, right, lower, corner, grad):
+    layers = right.shape[0]
+    pattern = corner.shape[-1]
+    modes = grad.shape[0]
+    anyw = pl.BlockSpec(memory_space=pl.ANY)
+    vmem = pl.BlockSpec(memory_space=pltpu.VMEM)
+    f32 = jnp.float32
+    half = (modes // 2, 2 * pattern, pattern)
+    dma = pltpu.SemaphoreType.DMA
+    count = modes // 2 + len(streams) * (2 * sum(way[2] - 1 for way in digits(rows, cols).values()) - 1)
+    from_left, from_above, total = pl.pallas_call(
+        functools.partial(share_kernel, rows, cols),
+        out_shape=(
+            jax.ShapeDtypeStruct(right.shape, f32),
+            jax.ShapeDtypeStruct(lower.shape, f32),
+            jax.ShapeDtypeStruct((modes, 2 * pattern, pattern), f32),
+        ),
+        in_specs=[anyw, anyw, anyw, vmem],
+        out_specs=(anyw, anyw, vmem),
+        scratch_shapes=[
+            pltpu.VMEM(right.shape, f32),
+            pltpu.VMEM(corner.shape, f32),
+            pltpu.VMEM(half, f32), pltpu.VMEM(half, f32), pltpu.VMEM(half, f32),
+            dma((1,)), dma((count,)), dma((count,)), dma((4 * layers,)), dma((4 * layers,)),
+        ],
+        compiler_params=pltpu.CompilerParams(
+            collective_id=1, has_side_effects=True, vmem_limit_bytes=40 * 1024 * 1024
+        ),
+        cost_estimate=pl.CostEstimate(flops=0, bytes_accessed=30_000_000, transcendentals=0),
+    )(right, lower, corner, grad.reshape(modes, 2 * pattern, pattern))
+    return from_left, from_above, total.reshape(grad.shape)
+
+
 def light_kernel(height, width, slots, info, probe, light, canvas, power):
     modes, _, pattern, _ = probe.shape
     total = jnp.zeros((pattern, pattern), jnp.float32)
@@ -251,15 +652,16 @@
     )(info, probe)
 
 
-def final_kernel(tile, grad, left, above, corner, light, out):
+def final_kernel(there, tile, grad, left, above, light, out):
     pattern = left.shape[-1]
-    grad[0, 0, :, :pattern] = grad[0, 0, :, :pattern] + left[0, 0]
-    grad[0, 0, :pattern, :] = grad[0, 0, :pattern, :] + above[0, 0]
-    grad[0, 0, :pattern, :pattern] = grad[0, 0, :pattern, :pattern] + corner[0, 0]
+    from_left = jnp.where(there[1] > 0, left[0, 0], 0.0)
+    from_above = jnp.where(there[0] > 0, above[0, 0], 0.0)
+    grad[0, 0, :, :pattern] = grad[0, 0, :, :pattern] + from_left
+    grad[0, 0, :pattern, :] = grad[0, 0, :pattern, :] + from_above
     out[0, 0] = tile[0, 0] - grad[0, 0] / light[...]
 
 
-def run_final(tile, grad, left, above, corner, light):
+def run_final(there, tile, grad, left, above, light):
     layers, parts, height, width = tile.shape
     spec = lambda array: pl.BlockSpec((1, 1) + array.shape[2:], lambda i, j: (i, j, 0, 0))
     return pl.pallas_call(
@@ -267,13 +669,14 @@
         grid=(layers, parts),
         out_shape=jax.ShapeDtypeStruct(tile.shape, jnp.float32),
         in_specs=[
-            spec(tile), spec(grad), spec(left), spec(above), spec(corner),
+            pl.BlockSpec(memory_space=pltpu.SMEM),
+            spec(tile), spec(grad), spec(left), spec(above),
             pl.BlockSpec(light.shape, lambda i, j: (0, 0)),
         ],
         out_specs=spec(tile),
         compiler_params=pltpu.CompilerParams(vmem_limit_bytes=24 * 1024 * 1024),
         cost_estimate=pl.CostEstimate(flops=4_000_000, bytes_accessed=14_000_000, transcendentals=0),
-    )(tile, grad, left, above, corner, light)
+    )(there, tile, grad, left, above, light)
 
 
 def on_device(object_slab, probe_mode_stack, offsets, measured, counts):
@@ -282,9 +685,8 @@
     pattern = probe_mode_stack.shape[-1]
     slots = offsets.shape[0]
     table_f, table_b, hop_f, hop_b = tables(pattern)
-    right_rim = from_behind(object_slab[:, :, :, :pattern], "scan", -1)
-    lower_rim = from_behind(object_slab[:, :, :pattern, :], "obj", -1)
-    corner_rim = from_behind(right_rim[:, :, :pattern, :], "obj", -1)
+    rows, cols = lax.axis_size("obj"), lax.axis_size("scan")
+    right_rim, lower_rim, corner_rim = run_rims(rows, cols, object_slab, pattern)
     base = jnp.stack([lax.axis_index("obj") * tile_height, lax.axis_index("scan") * tile_width])
     base = base.astype(jnp.int32)
     corners = offsets - base
@@ -301,13 +703,8 @@
         corners, counts, object_slab, right_rim, lower_rim, corner_rim, probe_mode_stack,
         measured, table_f, table_b, hop_f, hop_b,
     )
-    summed = lax.psum(grad_probe, ("obj", "scan"))
-    corner_half = from_behind(grad_corner, "obj", 1)
-    from_above = from_behind(grad_lower, "obj", 1)
-    from_left = from_behind(grad_right, "scan", 1)
-    from_corner = from_behind(corner_half, "scan", 1)
-    new_object = run_final(object_slab, grad_tile, from_left, from_above, from_corner, light)
-    summed, new_object = lax.optimization_barrier((summed, new_object))
+    from_left, from_above, summed = run_share(rows, cols, grad_right, grad_lower, grad_corner, grad_probe)
+    new_object = run_final(base, object_slab, grad_tile, from_left, from_above, light)
     grad_scale = jnp.sqrt(jnp.mean(summed * summed) + 1e-06)
     new_probe = probe_mode_stack - probe_step * summed / grad_scale
     return (new_object, new_probe)

time: 287 us -> 210 us (0.73)
  waiting for transfers between devices: 156 us -> 1 us
  Pallas kernels: 31.6 us -> 180 us
  starting transfers between devices: 63 us -> 5.02 us
  between operations: 15.6 us -> 2.16 us
  local copies, waits for them, and re-layouts: 7.68 us -> 13.2 us
  other arithmetic: 8.25 us -> 4.74 us
    pallas_call x0 -> x2, Pallas kernels: none -> 123 us  [the longest x1 80.6 us: run_share(): pl.pallas_call(functools.partial(share_kernel, rows, cols), out_shape=(ja...]
    ppermute x9 -> x2, waiting for transfers between devices: 81.2 us -> 1 us  [from_behind(): return lax.ppermute(array, axis, pairs)]
    psum x1 -> x0, waiting for transfers between devices: 74.7 us -> none  [on_device(): summed = lax.psum(grad_probe, ('obj', 'scan'))]
    ppermute x9 -> x2, starting transfers between devices: 62.9 us -> 5.02 us  [from_behind(): return lax.ppermute(array, axis, pairs)]
    pallas_call x1, Pallas kernels: 23.8 us -> 49.7 us  [run_slots(): pl.pallas_call(slots_kernel, out_shape=(jax.ShapeDtypeStruct(tile.shape,...]
    unnamed x17 -> x27, local copies, waits for them, and re-layouts: 4.2 us -> 12.9 us
    slice x3 -> x0, local copies, waits for them, and re-layouts: 3.22 us -> none  [the longest x1 1.66 us: on_device(): right_rim = from_behind(object_slab[:, :, :, :pattern], 'scan', -1)]
  transfers between devices with their start and end apart: 10 -> 2, of which waited for: 7 -> 1; matrix products, arithmetic and copies ran while one was open for 1% -> 0% of each run, Pallas kernels for 3% -> 21%
where the time goes in v2:
time: 210 us; the launch traced here: 206 us
  Pallas kernels  180 us (86%)
  local copies, waits for them, and re-layouts  13.2 us (6%)
  starting transfers between devices  5.02 us (2%)
  other arithmetic  4.74 us (2%)
  between operations  2.16 us (1%)
    pallas_call x1, Pallas kernels, run_share(): pl.pallas_call(functools.partial(share_kernel, rows, cols), out_shape=(ja...  80.6 us
    pallas_call x1, Pallas kernels, run_slots(): pl.pallas_call(slots_kernel, out_shape=(jax.ShapeDtypeStruct(tile.shape,...  49.7 us
    pallas_call x1, Pallas kernels, run_rims(): pl.pallas_call(functools.partial(rims_kernel, rows, cols), out_shape=(jax...  42.5 us
    unnamed x27, local copies, waits for them, and re-layouts  12.9 us
    ppermute x2, starting transfers between devices, from_behind(): return lax.ppermute(array, axis, pairs)  5.02 us
  transfers between devices with their start and end apart: 2, of which 1 were waited for; matrix products, arithmetic and copies ran while one was open for 0% of the time, Pallas kernels for 21%

profile of v2, /device:TPU:17, one launch (start us, length us, event | category | flops | bytes accessed | tf_op | source)
XLA Modules:
  0.0 205.8 jit_solution(944749642680662128)
XLA Ops:
  0.6 0.0 copy-start.1
  0.6 0.9 copy.13
  2.2 0.1 reshape.17
  2.3 0.1 pad_add_fusion.1
  2.4 3.1 %collective-permute-start = (s32[7]{0:T(128)S(1)}, s32[7]{0:T(128)S(1)}, u32[]{:S(2)}, u32[]{:S(2)}) collective-permute-start(s32[7]{0:T(128)S(1)} %pad_add_fusion.1), channel_id=1, source_target_pairs={{0,1},{1,2},{2,3},{3,4},{4,5},{5,6},{6,7},{8,9},{9,10},{10,11},{11... | collective-permute-start | bytes 92 | tf_op jit(solution)/shard_map/ppermute | solution.py:22
  5.5 42.5 %shard_map.104 = (f32[2,2,384,256]{3,2,1,0:T(8,128)}, f32[2,2,256,512]{3,2,1,0:T(8,128)}, f32[2,2,256,256]{3,2,1,0:T(8,128)}) custom-call(f32[2,2,384,512]{3,2,1,0:T(8,128)} %tile.24), custom_call_target="tpu_custom_call" | custom-call | bytes 10000000 | tf_op jit(solution)/shard_map/pallas_call | solution.py:326
  48.0 0.1 pad_add_fusion.there
  48.1 0.6 broadcast_subtract_fusion.corners
  48.7 0.1 tile.9
  48.8 0.1 pad_add_fusion.4
  48.9 0.0 collective-permute-done
  48.9 0.1 pad_add_fusion.2
  48.9 1.9 collective-permute-start.1
  50.9 0.1 tile.21
  50.9 1.0 collective-permute-done.1
  51.9 0.1 pad_add_fusion.3
  52.0 0.0 copy-done.1
  52.0 3.7 %shard_map.107.light = f32[384,512]{1,0:T(8,128)S(1)} custom-call(s32[28]{0:T(128)S(1)} %sub.16.info, f32[6,2,256,256]{3,2,1,0:T(8,128)S(1)} %copy-done.1), custom_call_target="tpu_custom_call" | custom-call | flops 10000000 | bytes 12000000 | tf_op jit(solution)/shard_map/pallas_call | solution.py:641
  55.7 0.0 copy-start.4
  55.7 0.9 copy-done.4
  56.6 49.7 %shard_map.105 = (f32[2,2,384,512]{3,2,1,0:T(8,128)}, f32[2,2,384,256]{3,2,1,0:T(8,128)}, f32[2,2,256,512]{3,2,1,0:T(8,128)}, f32[2,2,256,256]{3,2,1,0:T(8,128)}, f32[6,2,256,256]{3,2,1,0:T(8,128)}) custom-call(s32[3,2]{1,0:T(4,128)} %broadcast_subtract_fusion.corners, s32[1]{0:T(128)S(6)} %copy.15.used, f32[2,2,384,512]{3,2,1,0:T(8,128)} %tile.24, ...), custom_call_target="tpu_custom_call" | custom-call | flops 28999999488 | bytes 30000000 | tf_op jit(solution)/shard_map/pallas_call | solution.py:189
  106.3 0.0 copy-start.8
  106.3 1.6 copy-done.8
  107.9 0.0 copy-start.11
  107.9 1.4 copy-done.11
  109.3 0.0 copy-start.12
  109.3 1.2 copy-done.12
  110.5 80.6 %shard_map.106 = (f32[2,2,384,256]{3,2,1,0:T(8,128)S(1)}, f32[2,2,256,512]{3,2,1,0:T(8,128)S(1)}, f32[6,512,256]{2,1,0:T(8,128)S(1)}) custom-call(f32[2,2,384,256]{3,2,1,0:T(8,128)S(1)} %copy-done.11, f32[2,2,256,512]{3,2,1,0:T(8,128)S(1)} %copy-done.8, f32[2,2,256,256]{3,2,1,0:T(8,128)S(1)} %copy-done.12, f32[6,512,256]{2,1,0:T(8,128)} %bitcast.5), custom_call_target="tpu_custom_call" | custom-call | bytes 30000000 | tf_op jit(solution)/shard_map/pallas_call | solution.py:595
  191.1 0.0 copy-start.6
  191.1 1.3 copy-done.6
  192.5 0.0 copy-start.9
  192.5 1.2 copy-done.9
  193.6 1.4 multiply_reduce_fusion
  195.7 0.0 copy-start.2
  195.7 0.0 copy-start.10
  195.8 0.3 multiply_divide_fusion
  196.1 1.6 copy-done.2
  197.6 0.0 copy-start
  197.6 0.0 copy-start.3
  197.6 0.0 copy-start.5
  197.6 0.0 copy-start.7
  197.6 2.1 %sub.17 = f32[6,2,256,256]{3,2,1,0:T(8,128)} subtract(f32[6,2,256,256]{3,2,1,0:T(8,128)S(1)} %copy-done.2, f32[6,2,256,256]{3,2,1,0:T(8,128)S(1)} %bitcast.4) | non-fusion elementwise | flops 786432 | bytes 9437184 | tf_op jit(solution)/shard_map/sub | solution.py:709
  199.7 0.0 copy-done.10
  199.7 1.1 copy-done
  200.8 0.9 copy-done.3
  201.7 0.1 copy-done.5
  201.8 0.7 copy-done.7
  202.5 3.3 %shard_map.108 = f32[2,2,384,512]{3,2,1,0:T(8,128)} custom-call(s32[2]{0:T(128)S(1)} %pad_add_fusion.there, f32[2,2,384,512]{3,2,1,0:T(8,128)S(1)} %copy-done, f32[2,2,384,512]{3,2,1,0:T(8,128)S(1)} %copy-done.3, f32[2,2,384,256]{3,2,1,0:T(8,128)S(1)} %copy-done.10, f32[2,2,256,512]{3,2,1,0:T(8,128)S(1)} %copy-done.7, f32[384,512]{1,0:T(8,128)S(1)} %copy-done.5), custom_call_target="tpu_custom_call" | custom-call | flops 4000000 | bytes 14000000 | tf_op jit(solution)/shard_map/pallas_call | solution.py:667
  (3 shorter events, 0.0 us)
Async XLA Ops:
  0.6 51.4 %copy-start.1 = (f32[6,2,256,256]{3,2,1,0:T(8,128)S(1)}, f32[6,2,256,256]{3,2,1,0:T(8,128)}, u32[]{:S(2)}) copy-start(f32[6,2,256,256]{3,2,1,0:T(8,128)} %probe.3) | copy-start | bytes 9437188
  2.4 46.5 %collective-permute-start = (s32[7]{0:T(128)S(1)}, s32[7]{0:T(128)S(1)}, u32[]{:S(2)}, u32[]{:S(2)}) collective-permute-start(s32[7]{0:T(128)S(1)} %pad_add_fusion.1), channel_id=1, source_target_pairs={{0,1},{1,2},{2,3},{3,4},{4,5},{5,6},{6,7},{8,9},{9,10},{10,11},{11... | collective-permute-start | bytes 92 | tf_op jit(solution)/shard_map/ppermute | solution.py:22
  48.9 3.0 %collective-permute-start.1 = (s32[14]{0:T(128)S(1)}, s32[14]{0:T(128)S(1)}, u32[]{:S(2)}, u32[]{:S(2)}) collective-permute-start(s32[14]{0:T(128)S(1)} %pad_add_fusion.2), channel_id=1, source_target_pairs={{0,8},{8,16},{16,24},{1,9},{9,17},{17,25},{2,10},{10,18},{18,26},{... | collective-permute-start | bytes 176 | tf_op jit(solution)/shard_map/ppermute | solution.py:22
  55.7 0.9 copy-start.4
  106.3 1.6 copy-start.8
  107.9 1.4 copy-start.11
  109.3 1.2 copy-start.12
  191.1 1.3 copy-start.6
  192.5 1.2 copy-start.9
  195.7 1.9 copy-start.2
  195.7 4.0 %copy-start.10 = (f32[2,2,384,256]{3,2,1,0:T(8,128)S(1)}, f32[2,2,384,256]{3,2,1,0:T(8,128)}, u32[]{:S(2)}) copy-start(f32[2,2,384,256]{3,2,1,0:T(8,128)} %copy-done.9) | copy-start | bytes 4718596
  197.6 3.1 %copy-start = (f32[2,2,384,512]{3,2,1,0:T(8,128)S(1)}, f32[2,2,384,512]{3,2,1,0:T(8,128)}, u32[]{:S(2)}) copy-start(f32[2,2,384,512]{3,2,1,0:T(8,128)} %tile.24) | copy-start | bytes 9437188
  197.6 4.1 %copy-start.3 = (f32[2,2,384,512]{3,2,1,0:T(8,128)S(1)}, f32[2,2,384,512]{3,2,1,0:T(8,128)}, u32[]{:S(2)}) copy-start(f32[2,2,384,512]{3,2,1,0:T(8,128)} %get-tuple-element.25.grad) | copy-start | bytes 9437188
  197.6 4.2 %copy-start.5 = (f32[384,512]{1,0:T(8,128)S(1)}, f32[384,512]{1,0:T(8,128)}, u32[]{:S(2)}) copy-start(f32[384,512]{1,0:T(8,128)} %copy-done.4) | copy-start | bytes 2359300
  197.6 4.9 %copy-start.7 = (f32[2,2,256,512]{3,2,1,0:T(8,128)S(1)}, f32[2,2,256,512]{3,2,1,0:T(8,128)}, u32[]{:S(2)}) copy-start(f32[2,2,256,512]{3,2,1,0:T(8,128)} %copy-done.6) | copy-start | bytes 6291460

commit v3 on v1

v3 whole, which is shorter than its diff:
```python
import functools
import math

import jax
import jax.numpy as jnp
import numpy as np
from jax import lax
from jax.experimental import pallas as pl
from jax.experimental.pallas import tpu as pltpu
from jax.sharding import PartitionSpec as P

chirp_scale = 24.0
probe_step = 0.15
lanes = 128
sublanes = 8


def dft_parts(pattern):
    indices = np.arange(pattern)
    angles = (indices[:, None] * indices[None, :] % pattern) * (2.0 * math.pi / pattern)
    parts = (np.cos(angles) / math.sqrt(pattern), np.sin(angles) / math.sqrt(pattern))
    return [part.astype(np.float32).astype(jnp.bfloat16).astype(np.float64) for part in parts]


def block_matrix(real_part, imag_part):
    upper = np.concatenate([real_part, -imag_part], axis=1)
    lower = np.concatenate([imag_part, real_part], axis=1)
    return jnp.asarray(np.concatenate([upper, lower], axis=0).astype(np.float32), jnp.bfloat16)


def tables(pattern):
    cos, sin = dft_parts(pattern)
    indices = np.arange(pattern)
    freqs = ((indices + pattern // 2) % pattern - pattern // 2) / pattern
    chirp = np.exp(-1j * math.pi * chirp_scale * freqs**2)
    hop = (cos + 1j * sin) @ (chirp[:, None] * (cos - 1j * sin))
    return (
        block_matrix(cos, -sin), block_matrix(cos, sin),
        block_matrix(hop.real, hop.imag), block_matrix(hop.real, -hop.imag),
    )


def aligned(row, col):
    row_base = pl.multiple_of(row // sublanes * sublanes, sublanes)
    col_base = pl.multiple_of(col // lanes * lanes, lanes)
    return row_base, col_base, row - row_base, col - col_base


def pad(array):
    array = jnp.concatenate([array, jnp.zeros((array.shape[0], lanes), jnp.float32)], axis=1)
    return jnp.concatenate([array, jnp.zeros((sublanes, array.shape[1]), jnp.float32)], axis=0)


def roll_down(array, rows, cols):
    return pltpu.roll(pltpu.roll(array, cols, 1), rows, 0)


def transform(real_part, imag_part, left, right):
    pattern = real_part.shape[0]
    stacked = jnp.concatenate([real_part.astype(jnp.bfloat16), imag_part.astype(jnp.bfloat16)], axis=0)
    half = jnp.dot(left, stacked, preferred_element_type=jnp.float32).astype(jnp.bfloat16)
    half = jnp.concatenate([half[:pattern], half[pattern:]], axis=1)
    full = jnp.dot(half, right, preferred_element_type=jnp.float32)
    return full[:, :pattern], full[:, pattern:]


MESH = pl.DeviceIdType.MESH


def place():
    return lax.axis_index("obj"), lax.axis_index("scan")


def greet(partners):
    barrier = pltpu.get_barrier_semaphore()
    for exists, device in partners:

        @pl.when(exists)
        def _(device=device):
            pl.semaphore_signal(barrier, inc=1, device_id=device, device_id_type=MESH)

    count = 0
    for exists, _ in partners:
        count = count + (1 if exists is True else jnp.where(exists, 1, 0))
    pl.semaphore_wait(barrier, count)


def neighbours(rows, cols):
    row, col = place()
    return {
        "up": (row > 0, (row - 1, col)),
        "down": (row < rows - 1, (row + 1, col)),
        "left": (col > 0, (row, col - 1)),
        "right": (col < cols - 1, (row, col + 1)),
    }


def digits(rows, cols):
    return {
        "core": ("obj", 1, 2),
        "y": ("obj", 2, rows // 2),
        "x": ("scan", 1, 2),
        "z": ("scan", 2, cols // 2),
    }


def member(digit, by):
    axis, stride, radix = digit
    row, col = place()
    at = row if axis == "obj" else col
    mine = at // stride % radix
    theirs = (mine + by) % radix
    there = at + (theirs - mine) * stride
    return mine, theirs, ((there, col) if axis == "obj" else (row, there))


def group(digit):
    return [(True, member(digit, by)[2]) for by in range(1, digit[2])]


streams = (
    (0, 0, 2, ("x", "y", "z")),
    (1, 0, 2, ("y", "x", "z")),
    (2, 0, 1, ("x", "z", "y")),
    (2, 1, 1, ("y", "z", "x")),
)


class Reduction:
    def __init__(self, rows, cols, grad, total, held, landed, core_in, sems):
        self.ways = digits(rows, cols)
        self.grad, self.total, self.held, self.landed, self.core_in = grad, total, held, landed, core_in
        self.sent, self.got = sems
        self.count = 0
        self.pending = []
        self.share = grad.shape[0] // 2
        self.state = [[0, grad.shape[1]] for _ in streams]
        self.waits = [[] for _ in streams]
        self.landing = [0 for _ in streams]

    def copy(self, source, target, device):
        k = self.count
        self.count += 1
        made = pltpu.make_async_remote_copy(
            src_ref=source, dst_ref=target, send_sem=self.sent.at[k], recv_sem=self.got.at[k],
            device_id=device, device_id_type=MESH,
        )
        made.start()
        self.pending.append(made)
        return made

    def core_send(self, k):
        mine, theirs, device = member(self.ways["core"], 1)
        self.core_waits = getattr(self, "core_waits", {})
        self.core_waits[k] = self.copy(self.grad.at[theirs * self.share + k], self.core_in.at[k], device)

    def core_add(self, k):
        mine, _, _ = member(self.ways["core"], 1)
        self.core_waits[k].wait_recv()
        self.held[k] = self.grad[mine * self.share + k] + self.core_in[k]

    def lanes_of(self, s):
        return pl.ds(streams[s][1] * lanes, streams[s][2] * lanes)

    def scatter_send(self, s, step):
        mode = streams[s][0]
        digit = self.ways[streams[s][3][step]]
        start, size = self.state[s]
        part = size // digit[2]
        self.waits[s] = []
        for by in range(1, digit[2]):
            _, theirs, device = member(digit, by)
            spot = self.landed.at[mode, pl.ds(self.landing[s], part), self.lanes_of(s)]
            source = self.held.at[mode, pl.ds(pl.multiple_of(start + theirs * part, sublanes), part), self.lanes_of(s)]
            self.waits[s].append((self.copy(source, spot, device), self.landing[s]))
            self.landing[s] += part

    def scatter_add(self, s, step):
        mode = streams[s][0]
        digit = self.ways[streams[s][3][step]]
        start, size = self.state[s]
        part = size // digit[2]
        if digit[2] > 1:
            mine, _, _ = member(digit, 1)
            start = start + mine * part
        self.state[s] = [start, part]
        span = pl.ds(pl.multiple_of(start, sublanes), part)
        value = self.held[mode, span, self.lanes_of(s)]
        for made, landing in self.waits[s]:
            made.wait_recv()
            value = value + self.landed[mode, pl.ds(landing, part), self.lanes_of(s)]
        if step == 2:
            own = member(self.ways["core"], 1)[0] * self.share + mode
            self.total[own, span, self.lanes_of(s)] = value
        else:
            self.held[mode, span, self.lanes_of(s)] = value

    def gather_send(self, s, step):
        mode = streams[s][0]
        digit = self.ways[streams[s][3][step]]
        start, size = self.state[s]
        own = member(self.ways["core"], 1)[0] * self.share + mode
        self.waits[s] = []
        for by in range(1, digit[2]):
            spot = self.total.at[own, pl.ds(pl.multiple_of(start, sublanes), size), self.lanes_of(s)]
            self.waits[s].append(self.copy(spot, spot, member(digit, by)[2]))

    def gather_wait(self, s, step):
        digit = self.ways[streams[s][3][step]]
        start, size = self.state[s]
        for made in self.waits[s]:
            made.wait_recv()
        if digit[2] > 1:
            start = start - member(digit, 1)[0] * size
        self.state[s] = [start, size * digit[2]]

    def core_share(self, s):
        mine, _, device = member(self.ways["core"], 1)
        spot = self.total.at[mine * self.share + streams[s][0], :, self.lanes_of(s)]
        self.waits[s] = [self.copy(spot, spot, device)]


def when(conditions, action):
    pl.when(functools.reduce(jnp.logical_and, conditions))(action)


def rims_kernel(rows, cols, tile, info, right, lower, corner, boxes, sent, got, sent_box, got_box, sem):
    near = neighbours(rows, cols)
    row, col = place()
    layers, pattern = tile.shape[0], corner.shape[-1]
    height = tile.shape[2]
    has_up, up = near["up"]
    has_down, down = near["down"]
    has_left, left = near["left"]
    has_right, far_right = near["right"]
    after = (jnp.logical_and(has_down, has_right), (row + 1, col + 1))
    before = (jnp.logical_and(has_up, has_left), (row - 1, col - 1))
    keep = pltpu.make_async_copy(info, boxes.at[0], sem.at[0])
    keep.start()
    greet(list(near.values()) + [after, before])

    def copy(source, target, k, device, sems=(sent, got)):
        return pltpu.make_async_remote_copy(
            src_ref=source, dst_ref=target, send_sem=sems[0].at[k], recv_sem=sems[1].at[k],
            device_id=device, device_id_type=MESH,
        )

    top, rest = pl.ds(0, pattern), pl.ds(pattern, height - pattern)
    first = pl.ds(0, pattern)
    each = range(layers)
    tops = [copy(tile.at[n, :, top, first], right.at[n, :, top], 4 * n, left) for n in each]
    rests = [copy(tile.at[n, :, rest, first], right.at[n, :, rest], 4 * n + 1, left) for n in each]
    lowers = [copy(tile.at[n, :, top], lower.at[n], 4 * n + 2, up) for n in each]
    corners = [copy(right.at[n, :, top], corner.at[n], 4 * n + 3, up) for n in each]
    tell = [
        (has_right, has_left, copy(info, boxes.at[1], 0, far_right, (sent_box, got_box))),
        (has_down, has_up, copy(info, boxes.at[2], 1, down, (sent_box, got_box))),
        (after[0], before[0], copy(info, boxes.at[3], 2, after[1], (sent_box, got_box))),
    ]
    for to, _, box in tell:
        when([to], box.start)
    for n in each:
        when([has_left], tops[n].start)
        when([has_up], lowers[n].start)
    for n in each:
        when([has_left], rests[n].start)
    keep.wait()
    for k, (to, there, box) in enumerate(tell):
        when([there], box.wait_recv)

        @pl.when(jnp.logical_not(there))
        def _(k=k):
            boxes[k + 1] = jnp.zeros(boxes.shape[1:], jnp.int32)

        when([to], box.wait_send)
    for n in each:
        when([has_right], tops[n].wait_recv)
        when([has_right, has_up], corners[n].start)
    for n in each:
        when([has_right], rests[n].wait_recv)
        when([has_right, has_down], corners[n].wait_recv)
        when([has_right, has_up], corners[n].wait_send)
        when([has_down], lowers[n].wait_recv)
        when([has_left], tops[n].wait_send)
        when([has_left], rests[n].wait_send)
        when([has_up], lowers[n].wait_send)


def run_rims(rows, cols, tile, info, pattern):
    layers, _, height, width = tile.shape
    anyw = pl.BlockSpec(memory_space=pl.ANY)
    vmem = pl.BlockSpec(memory_space=pltpu.VMEM)
    f32, dma = jnp.float32, pltpu.SemaphoreType.DMA
    return pl.pallas_call(
        functools.partial(rims_kernel, rows, cols),
        out_shape=(
            jax.ShapeDtypeStruct((layers, 2, height, pattern), f32),
            jax.ShapeDtypeStruct((layers, 2, pattern, width), f32),
            jax.ShapeDtypeStruct((layers, 2, pattern, pattern), f32),
            jax.ShapeDtypeStruct((4,) + info.shape, jnp.int32),
        ),
        in_specs=[anyw, vmem],
        out_specs=(anyw, anyw, anyw, vmem),
        scratch_shapes=[dma((4 * layers,)), dma((4 * layers,)), dma((3,)), dma((3,)), dma((1,))],
        compiler_params=pltpu.CompilerParams(collective_id=0, has_side_effects=True),
        cost_estimate=pl.CostEstimate(flops=0, bytes_accessed=10_000_000, transcendentals=0),
    )(tile, info)


def slots_kernel(
    rows, cols, boxes, offsets, used, tile, right, lower, corner, probe_in, measured_in, table_f_in, table_b_in, hop_f_in, hop_b_in,
    grad_tile, grad_right, grad_lower, grad_corner, grad, light,
    ext0, ext1, window, waves, far, back, term, canvas, probe, measured, table_f, table_b, hop_f, hop_b, intensity,
    sems_in, sems_out,
):
    bf16 = jnp.bfloat16
    modes, pattern = probe.shape[0], probe.shape[-1]
    slots = offsets.shape[0]
    height, width = tile.shape[2], tile.shape[3]
    wide, tall = pattern + lanes, pattern + sublanes
    exts = (ext0, ext1)
    row, col = place()
    first, second = pl.ds(0, pattern), pl.ds(pattern, pattern)

    def spots(n):
        return (
            exts[n].at[:, pl.ds(0, height), pl.ds(0, width)],
            exts[n].at[:, pl.ds(0, height), pl.ds(width, pattern)],
            exts[n].at[:, pl.ds(height, pattern), pl.ds(0, width)],
            exts[n].at[:, pl.ds(height, pattern), pl.ds(width, pattern)],
        )

    moves = [(probe_in, probe)]
    moves += [(array.at[0], spot) for array, spot in zip((tile, right, lower, corner), spots(0))]
    moves += [(hop_f_in, hop_f), (hop_b_in, hop_b)]
    moves += [(array.at[1], spot) for array, spot in zip((tile, right, lower, corner), spots(1))]
    moves += [(table_f_in, table_f), (table_b_in, table_b), (measured_in, measured)]
    loads = [pltpu.make_async_copy(a, b, sems_in.at[k]) for k, (a, b) in enumerate(moves)]
    for load in loads:
        load.start()

    canvas[...] = jnp.zeros_like(canvas)
    loads[0].wait()
    power = jnp.zeros((pattern, pattern), jnp.float32)
    for mode in range(modes):
        power = power + (probe[mode, 0] * probe[mode, 0] + probe[mode, 1] * probe[mode, 1])
    intensity[...] = power
    for block in range(4):

        @pl.loop(0, boxes[block, 0, 2 * slots])
        def _(slot, block=block):
            at_row = boxes[block, 0, 2 * slot] - row * height + height
            at_col = boxes[block, 0, 2 * slot + 1] - col * width + width
            row_base, col_base, row_shift, col_shift = aligned(at_row, at_col)
            at = (pl.ds(row_base, tall), pl.ds(col_base, wide))
            canvas[at] = canvas[at] + roll_down(pad(intensity[...]), row_shift, col_shift)

    light[...] = canvas[height : 2 * height, width : 2 * width] + 1.0

    def bases(slot):
        return aligned(offsets[slot, 0] - row * height, offsets[slot, 1] - col * width)

    def cut(n):
        @pl.loop(0, used[0])
        def _(slot):
            row_base, col_base, row_shift, col_shift = bases(slot)
            row_back = jnp.where(row_shift == 0, 0, tall - row_shift)
            col_back = jnp.where(col_shift == 0, 0, wide - col_shift)
            for part in range(2):
                block = exts[n][part, pl.ds(row_base, tall), pl.ds(col_base, wide)]
                window[slot, n, part] = roll_down(block, row_back, col_back)[:pattern, :pattern]

    def spread(n, slot):
        row_base, col_base, row_shift, col_shift = bases(slot)
        for part in range(2):
            at = (part, pl.ds(row_base, tall), pl.ds(col_base, wide))
            exts[n][at] = exts[n][at] + roll_down(pad(term[part]), row_shift, col_shift)

    def save(n):
        return [
            pltpu.make_async_copy(spot, target.at[n], sems_out.at[4 * n + k])
            for k, (spot, target) in enumerate(zip(spots(n), (grad_tile, grad_right, grad_lower, grad_corner)))
        ]

    for k in range(1, 7):
        loads[k].wait()
    cut(0)
    exts[0][...] = jnp.zeros_like(exts[0])

    @pl.loop(0, used[0])
    def _(slot):
        @pl.loop(0, modes, unroll=3)
        def _(mode):
            wr, wi = probe[mode, 0], probe[mode, 1]
            o_r, o_i = window[slot, 0, 0], window[slot, 0, 1]
            wr, wi = transform(o_r * wr - o_i * wi, o_r * wi + o_i * wr, hop_f[...], hop_b[...])
            waves[slot, mode, 0] = wr
            waves[slot, mode, 1] = wi

    for k in range(7, len(moves)):
        loads[k].wait()
    cut(1)
    exts[1][...] = jnp.zeros_like(exts[1])

    @pl.loop(0, used[0])
    def _(slot):
        intensity[...] = -measured[slot]
        term[...] = jnp.zeros_like(term)

        @pl.loop(0, modes, unroll=3)
        def _(mode):
            wr, wi = waves[slot, mode, 0], waves[slot, mode, 1]
            o_r, o_i = window[slot, 1, 0], window[slot, 1, 1]
            fr, fi = transform(o_r * wr - o_i * wi, o_r * wi + o_i * wr, table_f[...], table_b[...])
            far[mode, 0] = fr
            far[mode, 1] = fi
            intensity[...] += fr * fr + fi * fi

        @pl.loop(0, modes, unroll=3)
        def _(mode):
            gain = intensity[...]
            gr, gi = transform(gain * far[mode, 0], gain * far[mode, 1], table_b[...], table_f[...])
            wr, wi = waves[slot, mode, 0], waves[slot, mode, 1]
            term[0] += wr * gr + wi * gi
            term[1] += wr * gi - wi * gr
            o_r, o_i = window[slot, 1, 0], window[slot, 1, 1]
            back[slot, mode, 0] = (o_r * gr + o_i * gi).astype(bf16)
            back[slot, mode, 1] = (o_r * gi - o_i * gr).astype(bf16)

        spread(1, slot)

    saves = save(1)
    for one in saves:
        one.start()
    grad[...] = jnp.zeros_like(grad)

    @pl.loop(0, used[0])
    def _(slot):
        term[...] = jnp.zeros_like(term)

        @pl.loop(0, modes, unroll=3)
        def _(mode):
            gr, gi = transform(back[slot, mode, 0], back[slot, mode, 1], hop_b[...], hop_f[...])
            wr, wi = probe[mode, 0], probe[mode, 1]
            term[0] += wr * gr + wi * gi
            term[1] += wr * gi - wi * gr
            o_r, o_i = window[slot, 0, 0], window[slot, 0, 1]
            grad[mode, first] += o_r * gr + o_i * gi
            grad[mode, second] += o_r * gi - o_i * gr

        spread(0, slot)

    last = save(0)
    for one in last:
        one.start()
    for one in saves + last:
        one.wait()


def run_slots(rows, cols, boxes, offsets, used, tile, right, lower, corner, probe, measured, *matrices):
    layers, _, height, width = tile.shape
    modes, _, pattern, _ = probe.shape
    slots = offsets.shape[0]
    smem = pl.BlockSpec(memory_space=pltpu.SMEM)
    vmem = pl.BlockSpec(memory_space=pltpu.VMEM)
    anyw = pl.BlockSpec(memory_space=pl.ANY)
    f32, bf16 = jnp.float32, jnp.bfloat16
    space, dma = pltpu.VMEM, pltpu.SemaphoreType.DMA
    ext = (2, height + pattern, width + pattern)
    return pl.pallas_call(
        functools.partial(slots_kernel, rows, cols),
        out_shape=(
            jax.ShapeDtypeStruct(tile.shape, f32),
            jax.ShapeDtypeStruct(right.shape, f32),
            jax.ShapeDtypeStruct(lower.shape, f32),
            jax.ShapeDtypeStruct(corner.shape, f32),
            jax.ShapeDtypeStruct((modes, 2 * pattern, pattern), f32),
            jax.ShapeDtypeStruct((height, width), f32),
        ),
        in_specs=[smem, smem, smem] + [anyw] * 10,
        out_specs=(anyw, anyw, anyw, anyw, vmem, vmem),
        scratch_shapes=[
            space(ext, f32), space(ext, f32),
            space((slots, layers, 2, pattern, pattern), f32),
            space((slots, modes, 2, pattern, pattern), f32),
            space((modes, 2, pattern, pattern), f32),
            space((slots, modes, 2, pattern, pattern), bf16),
            space((2, pattern, pattern), f32),
            space((2 * height + pattern, 2 * width + pattern), f32),
            space(probe.shape, f32), space(measured.shape, f32),
            *[space((2 * pattern, 2 * pattern), bf16) for _ in range(4)],
            space((pattern, pattern), f32),
            dma((14,)), dma((8,)),
        ],
        compiler_params=pltpu.CompilerParams(vmem_limit_bytes=58 * 1024 * 1024),
        cost_estimate=pl.CostEstimate(flops=20_000_000_000, bytes_accessed=30_000_000, transcendentals=0),
    )(boxes, offsets, used, tile, right, lower, corner, probe, measured, *matrices)


def share_kernel(
    rows, cols, tile, right, lower, corner, grad_tile, grad, light, probe_in, new_object, total,
    side, inner, left_in, above_in, edge, held, landed, core_in, probe, sems_in, sent_halo, got_halo, sent, got,
):
    near = neighbours(rows, cols)
    ways = digits(rows, cols)
    partners = list(near.values())
    for digit in ways.values():
        partners += group(digit)
    layers, pattern = right.shape[0], corner.shape[-1]
    height, width = tile.shape[2], tile.shape[3]
    modes = grad.shape[0]
    each = range(layers)
    first, second = pl.ds(0, pattern), pl.ds(pattern, pattern)
    moves = [(right, side), (tile, new_object), (grad_tile, inner), (probe_in, probe)]
    loads = [pltpu.make_async_copy(a, b, sems_in.at[k]) for k, (a, b) in enumerate(moves)]
    for load in loads:
        load.start()
    greet(partners)
    has_up, up = near["up"]
    has_down, down = near["down"]
    has_left, _ = near["left"]
    has_right, far_right = near["right"]

    def copy(source, target, k, device):
        return pltpu.make_async_remote_copy(
            src_ref=source, dst_ref=target, send_sem=sent_halo.at[k], recv_sem=got_halo.at[k],
            device_id=device, device_id_type=MESH,
        )

    top, rest = pl.ds(0, pattern), pl.ds(pattern, height - pattern)
    tops = [copy(side.at[n, :, top], left_in.at[n, :, top], 4 * n, far_right) for n in each]
    rests = [copy(side.at[n, :, rest], left_in.at[n, :, rest], 4 * n + 1, far_right) for n in each]
    lowers = [copy(lower.at[n], above_in.at[n], 4 * n + 2, down) for n in each]
    corners = [copy(corner.at[n], edge.at[n], 4 * n + 3, down) for n in each]
    reduction = Reduction(rows, cols, grad, total, held, landed, core_in, (sent, got))

    def add_corner(n):
        @pl.when(jnp.logical_and(has_right, has_up))
        def _():
            corners[n].wait_recv()
            side[n, :, :pattern] = side[n, :, :pattern] + edge[n]

        when([has_right], tops[n].start)

    def finish(n):
        @pl.when(has_left)
        def _():
            rests[n].wait_recv()
            tops[n].wait_recv()

        @pl.when(jnp.logical_not(has_left))
        def _():
            left_in[n] = jnp.zeros(left_in.shape[1:], jnp.float32)

        when([has_up], lowers[n].wait_recv)

        @pl.when(jnp.logical_not(has_up))
        def _():
            above_in[n] = jnp.zeros(above_in.shape[1:], jnp.float32)

        inner[n, :, :, :pattern] += left_in[n]
        inner[n, :, :pattern, :] += above_in[n]
        for part in range(2):
            new_object[n, part] = new_object[n, part] - inner[n, part] / light[...]

    every = range(len(streams))
    for k in range(reduction.share):
        reduction.core_send(k)
    when([has_down, has_right], corners[0].start)
    when([has_down, has_right], corners[1].start)
    loads[0].wait()
    for k in range(reduction.share):
        reduction.core_add(k)
        for s in every:
            if streams[s][0] == k:
                reduction.scatter_send(s, 0)
    when([has_right], rests[0].start)
    when([has_right], rests[1].start)
    when([has_down], lowers[0].start)
    add_corner(0)
    add_corner(1)
    when([has_down], lowers[1].start)
    for step in range(3):
        for s in every:
            reduction.scatter_add(s, step)
            if step < 2:
                reduction.scatter_send(s, step + 1)
            else:
                reduction.gather_send(s, 2)
    for step in (2, 1, 0):
        for s in every:
            reduction.gather_wait(s, step)
            if step:
                reduction.gather_send(s, step - 1)
            else:
                reduction.core_share(s)
    loads[1].wait()
    loads[2].wait()
    finish(0)
    finish(1)
    for s in range(len(streams)):
        for made in reduction.waits[s]:
            made.wait_recv()
    for made in reduction.pending:
        made.wait_send()
    for n in each:
        when([has_right], rests[n].wait_send)
        when([has_right], tops[n].wait_send)
        when([has_down, has_right], corners[n].wait_send)
        when([has_down], lowers[n].wait_send)
    loads[3].wait()
    squares = jnp.zeros((pattern, pattern), jnp.float32)
    for mode in range(modes):
        squares = squares + (total[mode, first] * total[mode, first] + total[mode, second] * total[mode, second])
    count = modes * 2 * pattern * pattern
    scale = jnp.sqrt(jnp.broadcast_to(jnp.sum(squares), (pattern, pattern)) * (1.0 / count) + 1e-06)
    factor = probe_step / scale
    for mode in range(modes):
        total[mode, first] = probe[mode, 0] - factor * total[mode, first]
        total[mode, second] = probe[mode, 1] - factor * total[mode, second]


def run_share(rows, cols, tile, right, lower, corner, grad_tile, grad, light, probe):
    layers = right.shape[0]
    pattern = corner.shape[-1]
    modes = grad.shape[0]
    anyw = pl.BlockSpec(memory_space=pl.ANY)
    vmem = pl.BlockSpec(memory_space=pltpu.VMEM)
    f32, space, dma = jnp.float32, pltpu.VMEM, pltpu.SemaphoreType.DMA
    half = (modes // 2, 2 * pattern, pattern)
    count = modes // 2 + len(streams) * (2 * sum(way[2] - 1 for way in digits(rows, cols).values()) - 1)
    new_object, new_probe = pl.pallas_call(
        functools.partial(share_kernel, rows, cols),
        out_shape=(
            jax.ShapeDtypeStruct(tile.shape, f32),
            jax.ShapeDtypeStruct((modes, 2 * pattern, pattern), f32),
        ),
        in_specs=[anyw, anyw, anyw, anyw, anyw, vmem, vmem, anyw],
        out_specs=(vmem, vmem),
        scratch_shapes=[
            space(right.shape, f32), space(tile.shape, f32), space(right.shape, f32), space(lower.shape, f32),
            space(corner.shape, f32), space(half, f32), space(half, f32), space(half, f32), space(probe.shape, f32),
            dma((4,)), dma((4 * layers,)), dma((4 * layers,)), dma((count,)), dma((count,)),
        ],
        compiler_params=pltpu.CompilerParams(
            collective_id=1, has_side_effects=True, vmem_limit_bytes=40 * 1024 * 1024
        ),
        cost_estimate=pl.CostEstimate(flops=0, bytes_accessed=30_000_000, transcendentals=0),
    )(tile, right, lower, corner, grad_tile, grad, light, probe)
    return new_object, new_probe.reshape(probe.shape)


def on_device(object_slab, probe_mode_stack, offsets, measured, counts):
    pattern = probe_mode_stack.shape[-1]
    rows, cols = lax.axis_size("obj"), lax.axis_size("scan")
    info = jnp.concatenate([offsets.reshape(-1), counts])
    info = jnp.pad(info[None], ((0, sublanes - 1), (0, lanes - info.shape[0])))
    right, lower, corner, boxes = run_rims(rows, cols, object_slab, info, pattern)
    grad_tile, right, lower, corner, grad, light = run_slots(
        rows, cols, boxes, offsets, counts, object_slab, right, lower, corner, probe_mode_stack, measured, *tables(pattern)
    )
    return run_share(rows, cols, object_slab, right, lower, corner, grad_tile, grad, light, probe_mode_stack)


def solution(mesh):
    in_specs = (
        P(None, None, "obj", "scan"),
        P(),
        P(("obj", "scan"), None),
        P(("obj", "scan"), None, None),
        P(("obj", "scan")),
    )
    out_specs = (P(None, None, "obj", "scan"), P())
    return jax.shard_map(
        on_device, mesh=mesh, in_specs=in_specs, out_specs=out_specs, check_vma=False
    )
```

time: 287 us -> 188 us (0.66)
  waiting for transfers between devices: 156 us -> 0 us
  Pallas kernels: 31.6 us -> 174 us
  starting transfers between devices: 63 us -> 0 us
  between operations: 15.6 us -> 1.32 us
  other arithmetic: 8.25 us -> 0.08 us
    pallas_call x3, Pallas kernels: 31.6 us -> 174 us  [the longest x1 110 us: run_share(): pl.pallas_call(functools.partial(share_kernel, rows, cols), out_shape=(ja...]
    ppermute x9 -> x0, waiting for transfers between devices: 81.2 us -> none  [from_behind(): return lax.ppermute(array, axis, pairs)]
    psum x1 -> x0, waiting for transfers between devices: 74.7 us -> none  [on_device(): summed = lax.psum(grad_probe, ('obj', 'scan'))]
    ppermute x9 -> x0, starting transfers between devices: 62.9 us -> none  [from_behind(): return lax.ppermute(array, axis, pairs)]
    unnamed x17 -> x13, local copies, waits for them, and re-layouts: 4.2 us -> 9.45 us
    sub x3 -> x0, other arithmetic: 4.57 us -> none  [the longest x1 3.97 us: on_device(): new_probe = probe_mode_stack - probe_step * summed / grad_scale]
    reduce_sum x1 -> x0, other arithmetic: 3.3 us -> none  [on_device(): grad_scale = jnp.sqrt(jnp.mean(summed * summed) + 1e-06)]
    slice x3 -> x0, local copies, waits for them, and re-layouts: 3.22 us -> none  [the longest x1 1.66 us: on_device(): right_rim = from_behind(object_slab[:, :, :, :pattern], 'scan', -1)]
  transfers between devices with their start and end apart: 10 -> 0, of which waited for: 7 -> 0; matrix products, arithmetic and copies ran while one was open for 1% -> 0% of each run, Pallas kernels for 3% -> 0%
where the time goes in v3:
time: 188 us; the launch traced here: 185 us
  Pallas kernels  174 us (93%)
  local copies, waits for them, and re-layouts  10.1 us (5%)
    pallas_call x1, Pallas kernels, run_share(): pl.pallas_call(functools.partial(share_kernel, rows, cols), out_shape=(ja...  110 us
    pallas_call x1, Pallas kernels, run_rims(): pl.pallas_call(functools.partial(rims_kernel, rows, cols), out_shape=(jax...  40.2 us
    pallas_call x1, Pallas kernels, run_slots(): pl.pallas_call(functools.partial(slots_kernel, rows, cols), out_shape=(ja...  23.1 us
    unnamed x13, local copies, waits for them, and re-layouts  9.45 us

profile of v3, /device:TPU:17, one launch (start us, length us, event | category | flops | bytes accessed | tf_op | source)
XLA Modules:
  0.0 185.1 jit_solution(4672327814648470058)
XLA Ops:
  1.3 0.8 copy.13.offsets
  2.0 0.0 copy-start.4
  2.0 0.1 reshape.10
  2.1 0.1 add_bitcast_fusion
  2.2 0.6 pad.4.info
  2.8 40.2 %shard_map.104 = (f32[2,2,384,256]{3,2,1,0:T(8,128)}, f32[2,2,256,512]{3,2,1,0:T(8,128)}, f32[2,2,256,256]{3,2,1,0:T(8,128)}, s32[4,8,128]{2,1,0:T(8,128)}) custom-call(f32[2,2,384,512]{3,2,1,0:T(8,128)} %tile.5, s32[8,128]{1,0:T(8,128)} %pad.4.info), custom_call_target="tpu_custom_call" | custom-call | bytes 10000000 | tf_op jit(solution)/shard_map/pallas_call | solution.py:294
  43.0 0.0 copy-done.4
  43.0 23.1 %shard_map.105 = (f32[2,2,384,512]{3,2,1,0:T(8,128)}, f32[2,2,384,256]{3,2,1,0:T(8,128)}, f32[2,2,256,512]{3,2,1,0:T(8,128)}, f32[2,2,256,256]{3,2,1,0:T(8,128)}...) custom-call(s32[4,8,128]{2,1,0:T(8,128)} %get-tuple-element.14.boxes, s32[3,2]{1,0:T(4,128)} %copy-done.4, s32[1]{0:T(128)S(6)} %copy.17.used, ...), custom_call_target="tpu_custom_call" | custom-call | flops 20000000000 | bytes 30000000 | tf_op jit(solution)/shard_map/pallas_call | solution.py:470
  66.1 0.0 copy-start
  66.2 1.6 copy-done
  67.7 0.0 copy-start.1
  67.7 1.4 copy-done.1
  69.1 0.0 copy-start.2
  69.2 1.2 copy-done.2
  70.4 0.0 copy-start.3
  70.4 1.1 copy-done.3
  71.5 110.3 %shard_map.106 = (f32[2,2,384,512]{3,2,1,0:T(8,128)S(1)}, f32[6,512,256]{2,1,0:T(8,128)S(1)}) custom-call(f32[2,2,384,512]{3,2,1,0:T(8,128)} %tile.5, f32[2,2,384,256]{3,2,1,0:T(8,128)S(1)} %copy-done.1, f32[2,2,256,512]{3,2,1,0:T(8,128)S(1)} %copy-done, f32[2,2,256,256]{3,2,1,0:T(8,128)S(1)} %copy-done.2, f32[2,2,384,512]{3,2,1,0:T(8,128)} %get-tuple-element.21.grad_tile, ...), custom_call_target="tpu_custom_call" | custom-call | bytes 30000000 | tf_op jit(solution)/shard_map/pallas_call | solution.py:632
  181.8 1.7 copy.18
  183.5 1.7 copy.19
Async XLA Ops:
  2.0 40.9 %copy-start.4 = (s32[3,2]{1,0:T(4,128)}, s32[3,2]{1,0:T(4,128)S(1)}, u32[]{:S(2)}) copy-start(s32[3,2]{1,0:T(4,128)S(1)} %copy.13.offsets) | copy-start | bytes 76
  66.1 1.6 copy-start
  67.7 1.4 copy-start.1
  69.1 1.2 copy-start.2
  70.4 1.1 copy-start.3

commit v4 on v3

--- a/solution.py
+++ b/solution.py
@@ -567,36 +567,40 @@
     for k in range(reduction.share):
         reduction.core_send(k)
     when([has_down, has_right], corners[0].start)
-    when([has_down, has_right], corners[1].start)
     loads[0].wait()
+    when([has_right], rests[0].start)
     for k in range(reduction.share):
         reduction.core_add(k)
         for s in every:
             if streams[s][0] == k:
                 reduction.scatter_send(s, 0)
-    when([has_right], rests[0].start)
+    when([has_down, has_right], corners[1].start)
     when([has_right], rests[1].start)
+    for s in every:
+        reduction.scatter_add(s, 0)
+        reduction.scatter_send(s, 1)
+    add_corner(0)
     when([has_down], lowers[0].start)
-    add_corner(0)
+    for s in every:
+        reduction.scatter_add(s, 1)
+        reduction.scatter_send(s, 2)
+    for s in every:
+        reduction.scatter_add(s, 2)
+        reduction.gather_send(s, 2)
     add_corner(1)
     when([has_down], lowers[1].start)
-    for step in range(3):
-        for s in every:
-            reduction.scatter_add(s, step)
-            if step < 2:
-                reduction.scatter_send(s, step + 1)
-            else:
-                reduction.gather_send(s, 2)
-    for step in (2, 1, 0):
-        for s in every:
-            reduction.gather_wait(s, step)
-            if step:
-                reduction.gather_send(s, step - 1)
-            else:
-                reduction.core_share(s)
+    for s in every:
+        reduction.gather_wait(s, 2)
+        reduction.gather_send(s, 1)
     loads[1].wait()
     loads[2].wait()
+    for s in every:
+        reduction.gather_wait(s, 1)
+        reduction.gather_send(s, 0)
     finish(0)
+    for s in every:
+        reduction.gather_wait(s, 0)
+        reduction.core_share(s)
     finish(1)
     for s in range(len(streams)):
         for made in reduction.waits[s]:
@@ -643,7 +647,7 @@
             dma((4,)), dma((4 * layers,)), dma((4 * layers,)), dma((count,)), dma((count,)),
         ],
         compiler_params=pltpu.CompilerParams(
-            collective_id=1, has_side_effects=True, vmem_limit_bytes=40 * 1024 * 1024
+            collective_id=1, has_side_effects=True, vmem_limit_bytes=60 * 1024 * 1024
         ),
         cost_estimate=pl.CostEstimate(flops=0, bytes_accessed=30_000_000, transcendentals=0),
     )(tile, right, lower, corner, grad_tile, grad, light, probe)

time: 188 us -> 177 us (0.941); the launches traced: 185 us -> 177 us
  Pallas kernels: 174 us -> 168 us
  local copies, waits for them, and re-layouts: 10.1 us -> 7.14 us
    pallas_call x1, Pallas kernels: 110 us -> 103 us  [run_share(): pl.pallas_call(functools.partial(share_kernel, rows, cols), out_shape=(ja...]
    unnamed x13 -> x7, local copies, waits for them, and re-layouts: 9.45 us -> 6.46 us
where the time goes in v4:
time: 177 us
  Pallas kernels  168 us (95%)
  local copies, waits for them, and re-layouts  7.14 us (4%)
    pallas_call x1, Pallas kernels, run_share(): pl.pallas_call(functools.partial(share_kernel, rows, cols), out_shape=(ja...  103 us
    pallas_call x1, Pallas kernels, run_rims(): pl.pallas_call(functools.partial(rims_kernel, rows, cols), out_shape=(jax...  40.2 us
    pallas_call x1, Pallas kernels, run_slots(): pl.pallas_call(functools.partial(slots_kernel, rows, cols), out_shape=(ja...  24.4 us
    unnamed x7, local copies, waits for them, and re-layouts  6.46 us

profile of v4, /device:TPU:17, one launch (start us, length us, event | category | flops | bytes accessed | tf_op | source)
XLA Modules:
  0.0 176.6 jit_solution(1616779636971712860)
XLA Ops:
  1.3 0.8 copy.13.offsets
  2.0 0.0 copy-start.1
  2.0 0.1 reshape.10
  2.1 0.1 add_bitcast_fusion
  2.2 0.6 pad.4.info
  2.8 40.2 %shard_map.104 = (f32[2,2,384,256]{3,2,1,0:T(8,128)}, f32[2,2,256,512]{3,2,1,0:T(8,128)}, f32[2,2,256,256]{3,2,1,0:T(8,128)}, s32[4,8,128]{2,1,0:T(8,128)}) custom-call(f32[2,2,384,512]{3,2,1,0:T(8,128)} %tile.5, s32[8,128]{1,0:T(8,128)} %pad.4.info), custom_call_target="tpu_custom_call" | custom-call | bytes 10000000 | tf_op jit(solution)/shard_map/pallas_call | solution.py:294
  43.0 0.0 copy-done.1
  43.0 24.4 %shard_map.105 = (f32[2,2,384,512]{3,2,1,0:T(8,128)}, f32[2,2,384,256]{3,2,1,0:T(8,128)}, f32[2,2,256,512]{3,2,1,0:T(8,128)}, f32[2,2,256,256]{3,2,1,0:T(8,128)}...) custom-call(s32[4,8,128]{2,1,0:T(8,128)} %get-tuple-element.14.boxes, s32[3,2]{1,0:T(4,128)} %copy-done.1, s32[1]{0:T(128)S(6)} %copy.17.used, ...), custom_call_target="tpu_custom_call" | custom-call | flops 20000000000 | bytes 30000000 | tf_op jit(solution)/shard_map/pallas_call | solution.py:470
  67.4 103.5 %shard_map.106 = (f32[2,2,384,512]{3,2,1,0:T(8,128)}, f32[6,512,256]{2,1,0:T(8,128)}) custom-call(f32[2,2,384,512]{3,2,1,0:T(8,128)} %tile.5, f32[2,2,384,256]{3,2,1,0:T(8,128)} %get-tuple-element.18.right, f32[2,2,256,512]{3,2,1,0:T(8,128)} %get-tuple-element.19.lower, f32[2,2,256,256]{3,2,1,0:T(8,128)} %get-tuple-element.20.corner, ...), custom_call_target="tpu_custom_call" | custom-call | bytes 30000000 | tf_op jit(solution)/shard_map/pallas_call | solution.py:636
  170.9 0.0 copy-start
  170.9 4.0 %copy.18 = f32[2,2,384,512]{3,2,1,0:T(8,128)} copy(f32[2,2,384,512]{3,2,1,0:T(8,128)} %get-tuple-element.28) | data formatting | bytes 6291456
  174.9 0.0 copy-done
  174.9 1.7 copy.19
Async XLA Ops:
  2.0 40.9 %copy-start.1 = (s32[3,2]{1,0:T(4,128)}, s32[3,2]{1,0:T(4,128)S(1)}, u32[]{:S(2)}) copy-start(s32[3,2]{1,0:T(4,128)S(1)} %copy.13.offsets) | copy-start | bytes 76
  170.9 4.0 %copy-start = (f32[6,512,256]{2,1,0:T(8,128)S(1)}, f32[6,512,256]{2,1,0:T(8,128)}, u32[]{:S(2)}) copy-start(f32[6,512,256]{2,1,0:T(8,128)} %get-tuple-element.25) | copy-start | bytes 9437188

commit v5 on v4

--- a/solution.py
+++ b/solution.py
@@ -307,6 +307,14 @@
     )(tile, info)
 
 
+def each_mode(modes):
+    def run(body):
+        for mode in range(modes):
+            body(mode)
+
+    return run
+
+
 def slots_kernel(
     rows, cols, boxes, offsets, used, tile, right, lower, corner, probe_in, measured_in, table_f_in, table_b_in, hop_f_in, hop_b_in,
     grad_tile, grad_right, grad_lower, grad_corner, grad, light,
@@ -389,7 +397,7 @@
 
     @pl.loop(0, used[0])
     def _(slot):
-        @pl.loop(0, modes, unroll=3)
+        @each_mode(modes)
         def _(mode):
             wr, wi = probe[mode, 0], probe[mode, 1]
             o_r, o_i = window[slot, 0, 0], window[slot, 0, 1]
@@ -407,7 +415,7 @@
         intensity[...] = -measured[slot]
         term[...] = jnp.zeros_like(term)
 
-        @pl.loop(0, modes, unroll=3)
+        @each_mode(modes)
         def _(mode):
             wr, wi = waves[slot, mode, 0], waves[slot, mode, 1]
             o_r, o_i = window[slot, 1, 0], window[slot, 1, 1]
@@ -416,7 +424,7 @@
             far[mode, 1] = fi
             intensity[...] += fr * fr + fi * fi
 
-        @pl.loop(0, modes, unroll=3)
+        @each_mode(modes)
         def _(mode):
             gain = intensity[...]
             gr, gi = transform(gain * far[mode, 0], gain * far[mode, 1], table_b[...], table_f[...])
@@ -438,7 +446,7 @@
     def _(slot):
         term[...] = jnp.zeros_like(term)
 
-        @pl.loop(0, modes, unroll=3)
+        @each_mode(modes)
         def _(mode):
             gr, gi = transform(back[slot, mode, 0], back[slot, mode, 1], hop_b[...], hop_f[...])
             wr, wi = probe[mode, 0], probe[mode, 1]
@@ -528,10 +536,10 @@
         )
 
     top, rest = pl.ds(0, pattern), pl.ds(pattern, height - pattern)
-    tops = [copy(side.at[n, :, top], left_in.at[n, :, top], 4 * n, far_right) for n in each]
-    rests = [copy(side.at[n, :, rest], left_in.at[n, :, rest], 4 * n + 1, far_right) for n in each]
-    lowers = [copy(lower.at[n], above_in.at[n], 4 * n + 2, down) for n in each]
-    corners = [copy(corner.at[n], edge.at[n], 4 * n + 3, down) for n in each]
+    tops = [[copy(side.at[n, p, top], left_in.at[n, p, top], 6 * n + p, far_right) for p in (0, 1)] for n in each]
+    rests = [copy(side.at[n, :, rest], left_in.at[n, :, rest], 6 * n + 2, far_right) for n in each]
+    lowers = [[copy(lower.at[n, p], above_in.at[n, p], 6 * n + 3 + p, down) for p in (0, 1)] for n in each]
+    corners = [copy(corner.at[n], edge.at[n], 6 * n + 5, down) for n in each]
     reduction = Reduction(rows, cols, grad, total, held, landed, core_in, (sent, got))
 
     def add_corner(n):
@@ -540,19 +548,25 @@
             corners[n].wait_recv()
             side[n, :, :pattern] = side[n, :, :pattern] + edge[n]
 
-        when([has_right], tops[n].start)
+    def release(n, part):
+        when([has_right], tops[n][part].start)
+        when([has_down], lowers[n][part].start)
 
     def finish(n):
         @pl.when(has_left)
         def _():
             rests[n].wait_recv()
-            tops[n].wait_recv()
+            tops[n][0].wait_recv()
+            tops[n][1].wait_recv()
 
         @pl.when(jnp.logical_not(has_left))
         def _():
             left_in[n] = jnp.zeros(left_in.shape[1:], jnp.float32)
 
-        when([has_up], lowers[n].wait_recv)
+        @pl.when(has_up)
+        def _():
+            lowers[n][0].wait_recv()
+            lowers[n][1].wait_recv()
 
         @pl.when(jnp.logical_not(has_up))
         def _():
@@ -580,18 +594,20 @@
         reduction.scatter_add(s, 0)
         reduction.scatter_send(s, 1)
     add_corner(0)
-    when([has_down], lowers[0].start)
+    release(0, 0)
     for s in every:
         reduction.scatter_add(s, 1)
         reduction.scatter_send(s, 2)
+    release(0, 1)
     for s in every:
         reduction.scatter_add(s, 2)
         reduction.gather_send(s, 2)
     add_corner(1)
-    when([has_down], lowers[1].start)
+    release(1, 0)
     for s in every:
         reduction.gather_wait(s, 2)
         reduction.gather_send(s, 1)
+    release(1, 1)
     loads[1].wait()
     loads[2].wait()
     for s in every:
@@ -609,9 +625,10 @@
         made.wait_send()
     for n in each:
         when([has_right], rests[n].wait_send)
-        when([has_right], tops[n].wait_send)
         when([has_down, has_right], corners[n].wait_send)
-        when([has_down], lowers[n].wait_send)
+        for part in (0, 1):
+            when([has_right], tops[n][part].wait_send)
+            when([has_down], lowers[n][part].wait_send)
     loads[3].wait()
     squares = jnp.zeros((pattern, pattern), jnp.float32)
     for mode in range(modes):
@@ -644,7 +661,7 @@
         scratch_shapes=[
             space(right.shape, f32), space(tile.shape, f32), space(right.shape, f32), space(lower.shape, f32),
             space(corner.shape, f32), space(half, f32), space(half, f32), space(half, f32), space(probe.shape, f32),
-            dma((4,)), dma((4 * layers,)), dma((4 * layers,)), dma((count,)), dma((count,)),
+            dma((4,)), dma((6 * layers,)), dma((6 * layers,)), dma((count,)), dma((count,)),
         ],
         compiler_params=pltpu.CompilerParams(
             collective_id=1, has_side_effects=True, vmem_limit_bytes=60 * 1024 * 1024

time: 177 us -> 172 us (0.972)
  Pallas kernels: 168 us -> 163 us
    pallas_call x1, Pallas kernels: 24.4 us -> 20.9 us  [run_slots(): pl.pallas_call(functools.partial(slots_kernel, rows, cols), out_shape=(ja...]
where the time goes in v5:
time: 172 us; the launch traced here: 171 us
  Pallas kernels  163 us (95%)
  local copies, waits for them, and re-layouts  7.14 us (4%)
    pallas_call x1, Pallas kernels, run_share(): pl.pallas_call(functools.partial(share_kernel, rows, cols), out_shape=(ja...  102 us
    pallas_call x1, Pallas kernels, run_rims(): pl.pallas_call(functools.partial(rims_kernel, rows, cols), out_shape=(jax...  40.2 us
    pallas_call x1, Pallas kernels, run_slots(): pl.pallas_call(functools.partial(slots_kernel, rows, cols), out_shape=(ja...  20.9 us
    unnamed x7, local copies, waits for them, and re-layouts  6.46 us

profile of v5, /device:TPU:17, one launch (start us, length us, event | category | flops | bytes accessed | tf_op | source)
XLA Modules:
  0.0 171.4 jit_solution(838959112970247288)
XLA Ops:
  1.3 0.8 copy.13.offsets
  2.0 0.0 copy-start.1
  2.0 0.1 reshape.10
  2.1 0.1 add_bitcast_fusion
  2.2 0.6 pad.4.info
  2.8 40.2 %shard_map.104 = (f32[2,2,384,256]{3,2,1,0:T(8,128)}, f32[2,2,256,512]{3,2,1,0:T(8,128)}, f32[2,2,256,256]{3,2,1,0:T(8,128)}, s32[4,8,128]{2,1,0:T(8,128)}) custom-call(f32[2,2,384,512]{3,2,1,0:T(8,128)} %tile.5, s32[8,128]{1,0:T(8,128)} %pad.4.info), custom_call_target="tpu_custom_call" | custom-call | bytes 10000000 | tf_op jit(solution)/shard_map/pallas_call | solution.py:294
  43.0 0.0 copy-done.1
  43.0 20.9 %shard_map.105 = (f32[2,2,384,512]{3,2,1,0:T(8,128)}, f32[2,2,384,256]{3,2,1,0:T(8,128)}, f32[2,2,256,512]{3,2,1,0:T(8,128)}, f32[2,2,256,256]{3,2,1,0:T(8,128)}...) custom-call(s32[4,8,128]{2,1,0:T(8,128)} %get-tuple-element.14.boxes, s32[3,2]{1,0:T(4,128)} %copy-done.1, s32[1]{0:T(128)S(6)} %copy.17.used, ...), custom_call_target="tpu_custom_call" | custom-call | flops 20000000000 | bytes 30000000 | tf_op jit(solution)/shard_map/pallas_call | solution.py:478
  64.0 101.7 %shard_map.106 = (f32[2,2,384,512]{3,2,1,0:T(8,128)}, f32[6,512,256]{2,1,0:T(8,128)}) custom-call(f32[2,2,384,512]{3,2,1,0:T(8,128)} %tile.5, f32[2,2,384,256]{3,2,1,0:T(8,128)} %get-tuple-element.18.right, f32[2,2,256,512]{3,2,1,0:T(8,128)} %get-tuple-element.19.lower, f32[2,2,256,256]{3,2,1,0:T(8,128)} %get-tuple-element.20.corner, ...), custom_call_target="tpu_custom_call" | custom-call | bytes 30000000 | tf_op jit(solution)/shard_map/pallas_call | solution.py:653
  165.7 0.0 copy-start
  165.7 4.0 %copy.18 = f32[2,2,384,512]{3,2,1,0:T(8,128)} copy(f32[2,2,384,512]{3,2,1,0:T(8,128)} %get-tuple-element.28) | data formatting | bytes 6291456
  169.7 0.0 copy-done
  169.7 1.7 copy.19
Async XLA Ops:
  2.0 40.9 %copy-start.1 = (s32[3,2]{1,0:T(4,128)}, s32[3,2]{1,0:T(4,128)S(1)}, u32[]{:S(2)}) copy-start(s32[3,2]{1,0:T(4,128)S(1)} %copy.13.offsets) | copy-start | bytes 76
  165.7 4.0 %copy-start = (f32[6,512,256]{2,1,0:T(8,128)S(1)}, f32[6,512,256]{2,1,0:T(8,128)}, u32[]{:S(2)}) copy-start(f32[6,512,256]{2,1,0:T(8,128)} %get-tuple-element.25) | copy-start | bytes 9437188

commit v6 on v5

--- a/solution.py
+++ b/solution.py
@@ -317,8 +317,8 @@
 
 def slots_kernel(
     rows, cols, boxes, offsets, used, tile, right, lower, corner, probe_in, measured_in, table_f_in, table_b_in, hop_f_in, hop_b_in,
-    grad_tile, grad_right, grad_lower, grad_corner, grad, light,
-    ext0, ext1, window, waves, far, back, term, canvas, probe, measured, table_f, table_b, hop_f, hop_b, intensity,
+    grad_tile, grad_right, grad_lower, grad_corner, grad_out, light_out,
+    grad, light, ext0, ext1, window, waves, far, back, term, canvas, probe, measured, table_f, table_b, hop_f, hop_b, intensity,
     sems_in, sems_out,
 ):
     bf16 = jnp.bfloat16
@@ -364,6 +364,8 @@
             canvas[at] = canvas[at] + roll_down(pad(intensity[...]), row_shift, col_shift)
 
     light[...] = canvas[height : 2 * height, width : 2 * width] + 1.0
+    light_save = pltpu.make_async_copy(light, light_out, sems_out.at[8])
+    light_save.start()
 
     def bases(slot):
         return aligned(offsets[slot, 0] - row * height, offsets[slot, 1] - col * width)
@@ -382,7 +384,7 @@
         row_base, col_base, row_shift, col_shift = bases(slot)
         for part in range(2):
             at = (part, pl.ds(row_base, tall), pl.ds(col_base, wide))
-            exts[n][at] = exts[n][at] + roll_down(pad(term[part]), row_shift, col_shift)
+            exts[n][at] = exts[n][at] + roll_down(pad(term[slot, part]), row_shift, col_shift)
 
     def save(n):
         return [
@@ -413,7 +415,7 @@
     @pl.loop(0, used[0])
     def _(slot):
         intensity[...] = -measured[slot]
-        term[...] = jnp.zeros_like(term)
+        term[slot] = jnp.zeros(term.shape[1:], jnp.float32)
 
         @each_mode(modes)
         def _(mode):
@@ -429,8 +431,8 @@
             gain = intensity[...]
             gr, gi = transform(gain * far[mode, 0], gain * far[mode, 1], table_b[...], table_f[...])
             wr, wi = waves[slot, mode, 0], waves[slot, mode, 1]
-            term[0] += wr * gr + wi * gi
-            term[1] += wr * gi - wi * gr
+            term[slot, 0] += wr * gr + wi * gi
+            term[slot, 1] += wr * gi - wi * gr
             o_r, o_i = window[slot, 1, 0], window[slot, 1, 1]
             back[slot, mode, 0] = (o_r * gr + o_i * gi).astype(bf16)
             back[slot, mode, 1] = (o_r * gi - o_i * gr).astype(bf16)
@@ -444,24 +446,29 @@
 
     @pl.loop(0, used[0])
     def _(slot):
-        term[...] = jnp.zeros_like(term)
+        term[slot] = jnp.zeros(term.shape[1:], jnp.float32)
 
         @each_mode(modes)
         def _(mode):
             gr, gi = transform(back[slot, mode, 0], back[slot, mode, 1], hop_b[...], hop_f[...])
             wr, wi = probe[mode, 0], probe[mode, 1]
-            term[0] += wr * gr + wi * gi
-            term[1] += wr * gi - wi * gr
+            term[slot, 0] += wr * gr + wi * gi
+            term[slot, 1] += wr * gi - wi * gr
             o_r, o_i = window[slot, 0, 0], window[slot, 0, 1]
             grad[mode, first] += o_r * gr + o_i * gi
             grad[mode, second] += o_r * gi - o_i * gr
 
+    grad_save = pltpu.make_async_copy(grad, grad_out, sems_out.at[9])
+    grad_save.start()
+
+    @pl.loop(0, used[0])
+    def _(slot):
         spread(0, slot)
 
     last = save(0)
     for one in last:
         one.start()
-    for one in saves + last:
+    for one in saves + last + [light_save, grad_save]:
         one.wait()
 
 
@@ -486,19 +493,20 @@
             jax.ShapeDtypeStruct((height, width), f32),
         ),
         in_specs=[smem, smem, smem] + [anyw] * 10,
-        out_specs=(anyw, anyw, anyw, anyw, vmem, vmem),
+        out_specs=(anyw,) * 6,
         scratch_shapes=[
+            space((modes, 2 * pattern, pattern), f32), space((height, width), f32),
             space(ext, f32), space(ext, f32),
             space((slots, layers, 2, pattern, pattern), f32),
             space((slots, modes, 2, pattern, pattern), f32),
             space((modes, 2, pattern, pattern), f32),
             space((slots, modes, 2, pattern, pattern), bf16),
-            space((2, pattern, pattern), f32),
+            space((slots, 2, pattern, pattern), f32),
             space((2 * height + pattern, 2 * width + pattern), f32),
             space(probe.shape, f32), space(measured.shape, f32),
             *[space((2 * pattern, 2 * pattern), bf16) for _ in range(4)],
             space((pattern, pattern), f32),
-            dma((14,)), dma((8,)),
+            dma((14,)), dma((10,)),
         ],
         compiler_params=pltpu.CompilerParams(vmem_limit_bytes=58 * 1024 * 1024),
         cost_estimate=pl.CostEstimate(flops=20_000_000_000, bytes_accessed=30_000_000, transcendentals=0),
@@ -506,8 +514,8 @@
 
 
 def share_kernel(
-    rows, cols, tile, right, lower, corner, grad_tile, grad, light, probe_in, new_object, total,
-    side, inner, left_in, above_in, edge, held, landed, core_in, probe, sems_in, sent_halo, got_halo, sent, got,
+    rows, cols, tile, right, lower, corner, grad_tile, grad, light, probe_in, new_object, new_probe,
+    fresh, total, side, inner, left_in, above_in, edge, held, landed, core_in, probe, sems_in, sems_out, sent_halo, got_halo, sent, got,
 ):
     near = neighbours(rows, cols)
     ways = digits(rows, cols)
@@ -519,7 +527,7 @@
     modes = grad.shape[0]
     each = range(layers)
     first, second = pl.ds(0, pattern), pl.ds(pattern, pattern)
-    moves = [(right, side), (tile, new_object), (grad_tile, inner), (probe_in, probe)]
+    moves = [(right, side), (tile, fresh), (grad_tile, inner), (probe_in, probe)]
     loads = [pltpu.make_async_copy(a, b, sems_in.at[k]) for k, (a, b) in enumerate(moves)]
     for load in loads:
         load.start()
@@ -540,6 +548,8 @@
     rests = [copy(side.at[n, :, rest], left_in.at[n, :, rest], 6 * n + 2, far_right) for n in each]
     lowers = [[copy(lower.at[n, p], above_in.at[n, p], 6 * n + 3 + p, down) for p in (0, 1)] for n in each]
     corners = [copy(corner.at[n], edge.at[n], 6 * n + 5, down) for n in each]
+    leaves = [pltpu.make_async_copy(fresh.at[n], new_object.at[n], sems_out.at[n]) for n in each]
+    outs = [pltpu.make_async_copy(total.at[m], new_probe.at[m], sems_out.at[layers + m]) for m in range(modes)]
     reduction = Reduction(rows, cols, grad, total, held, landed, core_in, (sent, got))
 
     def add_corner(n):
@@ -575,7 +585,8 @@
         inner[n, :, :, :pattern] += left_in[n]
         inner[n, :, :pattern, :] += above_in[n]
         for part in range(2):
-            new_object[n, part] = new_object[n, part] - inner[n, part] / light[...]
+            fresh[n, part] = fresh[n, part] - inner[n, part] / light[...]
+        leaves[n].start()
 
     every = range(len(streams))
     for k in range(reduction.share):
@@ -618,27 +629,38 @@
         reduction.gather_wait(s, 0)
         reduction.core_share(s)
     finish(1)
+    mine, theirs, _ = member(ways["core"], 1)
+
+    def squares_of(half):
+        squares = jnp.zeros((pattern, pattern), jnp.float32)
+        for m in range(reduction.share):
+            mode = half * reduction.share + m
+            squares = squares + (total[mode, first] * total[mode, first] + total[mode, second] * total[mode, second])
+        return squares
+
+    squares = squares_of(mine)
     for s in range(len(streams)):
         for made in reduction.waits[s]:
             made.wait_recv()
+    squares = squares + squares_of(theirs)
     for made in reduction.pending:
         made.wait_send()
+    loads[3].wait()
+    count = modes * 2 * pattern * pattern
+    scale = jnp.sqrt(jnp.broadcast_to(jnp.sum(squares), (pattern, pattern)) * (1.0 / count) + 1e-06)
+    factor = probe_step / scale
+    for mode in range(modes):
+        total[mode, first] = probe[mode, 0] - factor * total[mode, first]
+        total[mode, second] = probe[mode, 1] - factor * total[mode, second]
+        outs[mode].start()
     for n in each:
         when([has_right], rests[n].wait_send)
         when([has_down, has_right], corners[n].wait_send)
         for part in (0, 1):
             when([has_right], tops[n][part].wait_send)
             when([has_down], lowers[n][part].wait_send)
-    loads[3].wait()
-    squares = jnp.zeros((pattern, pattern), jnp.float32)
-    for mode in range(modes):
-        squares = squares + (total[mode, first] * total[mode, first] + total[mode, second] * total[mode, second])
-    count = modes * 2 * pattern * pattern
-    scale = jnp.sqrt(jnp.broadcast_to(jnp.sum(squares), (pattern, pattern)) * (1.0 / count) + 1e-06)
-    factor = probe_step / scale
-    for mode in range(modes):
-        total[mode, first] = probe[mode, 0] - factor * total[mode, first]
-        total[mode, second] = probe[mode, 1] - factor * total[mode, second]
+    for one in leaves + outs:
+        one.wait()
 
 
 def run_share(rows, cols, tile, right, lower, corner, grad_tile, grad, light, probe):
@@ -657,11 +679,12 @@
             jax.ShapeDtypeStruct((modes, 2 * pattern, pattern), f32),
         ),
         in_specs=[anyw, anyw, anyw, anyw, anyw, vmem, vmem, anyw],
-        out_specs=(vmem, vmem),
+        out_specs=(anyw, anyw),
         scratch_shapes=[
+            space(tile.shape, f32), space((modes, 2 * pattern, pattern), f32),
             space(right.shape, f32), space(tile.shape, f32), space(right.shape, f32), space(lower.shape, f32),
             space(corner.shape, f32), space(half, f32), space(half, f32), space(half, f32), space(probe.shape, f32),
-            dma((4,)), dma((6 * layers,)), dma((6 * layers,)), dma((count,)), dma((count,)),
+            dma((4,)), dma((layers + modes,)), dma((6 * layers,)), dma((6 * layers,)), dma((count,)), dma((count,)),
         ],
         compiler_params=pltpu.CompilerParams(
             collective_id=1, has_side_effects=True, vmem_limit_bytes=60 * 1024 * 1024

time: 172 us -> 167 us (0.971)
  Pallas kernels: 163 us -> 159 us
    pallas_call x1, Pallas kernels: 102 us -> 97.6 us  [run_share(): pl.pallas_call(functools.partial(share_kernel, rows, cols), out_shape=(ja...]
where the time goes in v6:
time: 167 us
  Pallas kernels  159 us (95%)
  local copies, waits for them, and re-layouts  7.14 us (4%)
    pallas_call x1, Pallas kernels, run_share(): pl.pallas_call(functools.partial(share_kernel, rows, cols), out_shape=(ja...  97.6 us
    pallas_call x1, Pallas kernels, run_rims(): pl.pallas_call(functools.partial(rims_kernel, rows, cols), out_shape=(jax...  40.2 us
    pallas_call x1, Pallas kernels, run_slots(): pl.pallas_call(functools.partial(slots_kernel, rows, cols), out_shape=(ja...  20.9 us
    unnamed x7, local copies, waits for them, and re-layouts  6.46 us

profile of v6, /device:TPU:17, one launch (start us, length us, event | category | flops | bytes accessed | tf_op | source)
XLA Modules:
  0.0 167.2 jit_solution(16820958529909386056)
XLA Ops:
  1.3 0.8 copy.13.offsets
  2.0 0.0 copy-start.1
  2.0 0.1 reshape.10
  2.1 0.1 add_bitcast_fusion
  2.2 0.6 pad.4.info
  2.8 40.2 %shard_map.104 = (f32[2,2,384,256]{3,2,1,0:T(8,128)}, f32[2,2,256,512]{3,2,1,0:T(8,128)}, f32[2,2,256,256]{3,2,1,0:T(8,128)}, s32[4,8,128]{2,1,0:T(8,128)}) custom-call(f32[2,2,384,512]{3,2,1,0:T(8,128)} %tile.5, s32[8,128]{1,0:T(8,128)} %pad.4.info), custom_call_target="tpu_custom_call" | custom-call | bytes 10000000 | tf_op jit(solution)/shard_map/pallas_call | solution.py:294
  43.0 0.0 copy-done.1
  43.0 20.9 %shard_map.105 = (f32[2,2,384,512]{3,2,1,0:T(8,128)}, f32[2,2,384,256]{3,2,1,0:T(8,128)}, f32[2,2,256,512]{3,2,1,0:T(8,128)}, f32[2,2,256,256]{3,2,1,0:T(8,128)}...) custom-call(s32[4,8,128]{2,1,0:T(8,128)} %get-tuple-element.14.boxes, s32[3,2]{1,0:T(4,128)} %copy-done.1, s32[1]{0:T(128)S(6)} %copy.17.used, ...), custom_call_target="tpu_custom_call" | custom-call | flops 20000000000 | bytes 30000000 | tf_op jit(solution)/shard_map/pallas_call | solution.py:485
  63.9 97.6 %shard_map.106 = (f32[2,2,384,512]{3,2,1,0:T(8,128)}, f32[6,512,256]{2,1,0:T(8,128)}) custom-call(f32[2,2,384,512]{3,2,1,0:T(8,128)} %tile.5, f32[2,2,384,256]{3,2,1,0:T(8,128)} %get-tuple-element.18.right, f32[2,2,256,512]{3,2,1,0:T(8,128)} %get-tuple-element.19.lower, f32[2,2,256,256]{3,2,1,0:T(8,128)} %get-tuple-element.20.corner, ...), custom_call_target="tpu_custom_call" | custom-call | bytes 30000000 | tf_op jit(solution)/shard_map/pallas_call | solution.py:675
  161.5 0.0 copy-start
  161.5 4.0 %copy.18 = f32[2,2,384,512]{3,2,1,0:T(8,128)} copy(f32[2,2,384,512]{3,2,1,0:T(8,128)} %get-tuple-element.28) | data formatting | bytes 6291456
  165.5 0.0 copy-done
  165.5 1.7 copy.19
Async XLA Ops:
  2.0 40.9 %copy-start.1 = (s32[3,2]{1,0:T(4,128)}, s32[3,2]{1,0:T(4,128)S(1)}, u32[]{:S(2)}) copy-start(s32[3,2]{1,0:T(4,128)S(1)} %copy.13.offsets) | copy-start | bytes 76
  161.5 4.0 %copy-start = (f32[6,512,256]{2,1,0:T(8,128)S(1)}, f32[6,512,256]{2,1,0:T(8,128)}, u32[]{:S(2)}) copy-start(f32[6,512,256]{2,1,0:T(8,128)} %get-tuple-element.25) | copy-start | bytes 9437188

commit v7 on v6

--- a/solution.py
+++ b/solution.py
@@ -119,10 +119,10 @@
 
 
 streams = (
-    (0, 0, 2, ("x", "y", "z")),
-    (1, 0, 2, ("y", "x", "z")),
-    (2, 0, 1, ("x", "z", "y")),
-    (2, 1, 1, ("y", "z", "x")),
+    (0, 0, 1, ("z", "x", "y")),
+    (0, 1, 1, ("y", "z", "x")),
+    (1, 0, 2, ("x", "y", "z")),
+    (2, 0, 2, ("y", "x", "z")),
 )
 
 
@@ -609,21 +609,21 @@
     for s in every:
         reduction.scatter_add(s, 1)
         reduction.scatter_send(s, 2)
-    release(0, 1)
     for s in every:
         reduction.scatter_add(s, 2)
         reduction.gather_send(s, 2)
+    release(0, 1)
     add_corner(1)
-    release(1, 0)
     for s in every:
         reduction.gather_wait(s, 2)
         reduction.gather_send(s, 1)
-    release(1, 1)
+    release(1, 0)
     loads[1].wait()
     loads[2].wait()
     for s in every:
         reduction.gather_wait(s, 1)
         reduction.gather_send(s, 0)
+    release(1, 1)
     finish(0)
     for s in every:
         reduction.gather_wait(s, 0)

time: 167 us -> 166 us (level)
    pallas_call x1, Pallas kernels: 97.6 us -> 86.5 us  [run_share(): pl.pallas_call(functools.partial(share_kernel, rows, cols), out_shape=(ja...]
    pallas_call x1, Pallas kernels: 20.9 us -> 31.7 us  [run_slots(): pl.pallas_call(functools.partial(slots_kernel, rows, cols), out_shape=(ja...]
where the time goes in v7:
time: 166 us; the launch traced here: 167 us
  Pallas kernels  158 us (95%)
  local copies, waits for them, and re-layouts  7.14 us (4%)
    pallas_call x1, Pallas kernels, run_share(): pl.pallas_call(functools.partial(share_kernel, rows, cols), out_shape=(ja...  86.5 us
    pallas_call x1, Pallas kernels, run_rims(): pl.pallas_call(functools.partial(rims_kernel, rows, cols), out_shape=(jax...  40.2 us
    pallas_call x1, Pallas kernels, run_slots(): pl.pallas_call(functools.partial(slots_kernel, rows, cols), out_shape=(ja...  31.7 us
    unnamed x7, local copies, waits for them, and re-layouts  6.46 us

profile of v7, /device:TPU:17, one launch (start us, length us, event | category | flops | bytes accessed | tf_op | source)
XLA Modules:
  0.0 166.8 jit_solution(13747565234677369511)
XLA Ops:
  1.3 0.8 copy.13.offsets
  2.0 0.0 copy-start.1
  2.0 0.1 reshape.10
  2.1 0.1 add_bitcast_fusion
  2.2 0.6 pad.4.info
  2.8 40.2 %shard_map.104 = (f32[2,2,384,256]{3,2,1,0:T(8,128)}, f32[2,2,256,512]{3,2,1,0:T(8,128)}, f32[2,2,256,256]{3,2,1,0:T(8,128)}, s32[4,8,128]{2,1,0:T(8,128)}) custom-call(f32[2,2,384,512]{3,2,1,0:T(8,128)} %tile.5, s32[8,128]{1,0:T(8,128)} %pad.4.info), custom_call_target="tpu_custom_call" | custom-call | bytes 10000000 | tf_op jit(solution)/shard_map/pallas_call | solution.py:294
  43.0 0.0 copy-done.1
  43.0 31.7 %shard_map.105 = (f32[2,2,384,512]{3,2,1,0:T(8,128)}, f32[2,2,384,256]{3,2,1,0:T(8,128)}, f32[2,2,256,512]{3,2,1,0:T(8,128)}, f32[2,2,256,256]{3,2,1,0:T(8,128)}...) custom-call(s32[4,8,128]{2,1,0:T(8,128)} %get-tuple-element.14.boxes, s32[3,2]{1,0:T(4,128)} %copy-done.1, s32[1]{0:T(128)S(6)} %copy.17.used, ...), custom_call_target="tpu_custom_call" | custom-call | flops 20000000000 | bytes 30000000 | tf_op jit(solution)/shard_map/pallas_call | solution.py:485
  74.7 86.5 %shard_map.106 = (f32[2,2,384,512]{3,2,1,0:T(8,128)}, f32[6,512,256]{2,1,0:T(8,128)}) custom-call(f32[2,2,384,512]{3,2,1,0:T(8,128)} %tile.5, f32[2,2,384,256]{3,2,1,0:T(8,128)} %get-tuple-element.18.right, f32[2,2,256,512]{3,2,1,0:T(8,128)} %get-tuple-element.19.lower, f32[2,2,256,256]{3,2,1,0:T(8,128)} %get-tuple-element.20.corner, ...), custom_call_target="tpu_custom_call" | custom-call | bytes 30000000 | tf_op jit(solution)/shard_map/pallas_call | solution.py:675
  161.2 0.0 copy-start
  161.2 4.0 %copy.18 = f32[2,2,384,512]{3,2,1,0:T(8,128)} copy(f32[2,2,384,512]{3,2,1,0:T(8,128)} %get-tuple-element.28) | data formatting | bytes 6291456
  165.2 0.0 copy-done
  165.2 1.7 copy.19
Async XLA Ops:
  2.0 40.9 %copy-start.1 = (s32[3,2]{1,0:T(4,128)}, s32[3,2]{1,0:T(4,128)S(1)}, u32[]{:S(2)}) copy-start(s32[3,2]{1,0:T(4,128)S(1)} %copy.13.offsets) | copy-start | bytes 76
  161.2 4.0 %copy-start = (f32[6,512,256]{2,1,0:T(8,128)S(1)}, f32[6,512,256]{2,1,0:T(8,128)}, u32[]{:S(2)}) copy-start(f32[6,512,256]{2,1,0:T(8,128)} %get-tuple-element.25) | copy-start | bytes 9437188

commit v8 on v7

--- a/solution.py
+++ b/solution.py
@@ -609,10 +609,10 @@
     for s in every:
         reduction.scatter_add(s, 1)
         reduction.scatter_send(s, 2)
+    release(0, 1)
     for s in every:
         reduction.scatter_add(s, 2)
         reduction.gather_send(s, 2)
-    release(0, 1)
     add_corner(1)
     for s in every:
         reduction.gather_wait(s, 2)

time: 166 us -> 168 us (1.012)
    pallas_call x1, Pallas kernels: 31.7 us -> 43.5 us  [run_slots(): pl.pallas_call(functools.partial(slots_kernel, rows, cols), out_shape=(ja...]
    pallas_call x1, Pallas kernels: 86.5 us -> 75.5 us  [run_share(): pl.pallas_call(functools.partial(share_kernel, rows, cols), out_shape=(ja...]
where the time goes in v8:
time: 168 us
  Pallas kernels  159 us (95%)
  local copies, waits for them, and re-layouts  7.14 us (4%)
    pallas_call x1, Pallas kernels, run_share(): pl.pallas_call(functools.partial(share_kernel, rows, cols), out_shape=(ja...  75.5 us
    pallas_call x1, Pallas kernels, run_slots(): pl.pallas_call(functools.partial(slots_kernel, rows, cols), out_shape=(ja...  43.5 us
    pallas_call x1, Pallas kernels, run_rims(): pl.pallas_call(functools.partial(rims_kernel, rows, cols), out_shape=(jax...  40.2 us
    unnamed x7, local copies, waits for them, and re-layouts  6.46 us

profile of v8, /device:TPU:17, one launch (start us, length us, event | category | flops | bytes accessed | tf_op | source)
XLA Modules:
  0.0 167.8 jit_solution(2817594178900564974)
XLA Ops:
  1.3 0.8 copy.13.offsets
  2.0 0.0 copy-start.1
  2.0 0.1 reshape.10
  2.1 0.1 add_bitcast_fusion
  2.2 0.6 pad.4.info
  2.8 40.2 %shard_map.104 = (f32[2,2,384,256]{3,2,1,0:T(8,128)}, f32[2,2,256,512]{3,2,1,0:T(8,128)}, f32[2,2,256,256]{3,2,1,0:T(8,128)}, s32[4,8,128]{2,1,0:T(8,128)}) custom-call(f32[2,2,384,512]{3,2,1,0:T(8,128)} %tile.5, s32[8,128]{1,0:T(8,128)} %pad.4.info), custom_call_target="tpu_custom_call" | custom-call | bytes 10000000 | tf_op jit(solution)/shard_map/pallas_call | solution.py:294
  43.0 0.0 copy-done.1
  43.0 43.5 %shard_map.105 = (f32[2,2,384,512]{3,2,1,0:T(8,128)}, f32[2,2,384,256]{3,2,1,0:T(8,128)}, f32[2,2,256,512]{3,2,1,0:T(8,128)}, f32[2,2,256,256]{3,2,1,0:T(8,128)}...) custom-call(s32[4,8,128]{2,1,0:T(8,128)} %get-tuple-element.14.boxes, s32[3,2]{1,0:T(4,128)} %copy-done.1, s32[1]{0:T(128)S(6)} %copy.17.used, ...), custom_call_target="tpu_custom_call" | custom-call | flops 20000000000 | bytes 30000000 | tf_op jit(solution)/shard_map/pallas_call | solution.py:485
  86.5 75.5 %shard_map.106 = (f32[2,2,384,512]{3,2,1,0:T(8,128)}, f32[6,512,256]{2,1,0:T(8,128)}) custom-call(f32[2,2,384,512]{3,2,1,0:T(8,128)} %tile.5, f32[2,2,384,256]{3,2,1,0:T(8,128)} %get-tuple-element.18.right, f32[2,2,256,512]{3,2,1,0:T(8,128)} %get-tuple-element.19.lower, f32[2,2,256,256]{3,2,1,0:T(8,128)} %get-tuple-element.20.corner, ...), custom_call_target="tpu_custom_call" | custom-call | bytes 30000000 | tf_op jit(solution)/shard_map/pallas_call | solution.py:675
  162.1 0.0 copy-start
  162.1 4.0 %copy.18 = f32[2,2,384,512]{3,2,1,0:T(8,128)} copy(f32[2,2,384,512]{3,2,1,0:T(8,128)} %get-tuple-element.28) | data formatting | bytes 6291456
  166.1 0.0 copy-done
  166.1 1.7 copy.19
Async XLA Ops:
  2.0 40.9 %copy-start.1 = (s32[3,2]{1,0:T(4,128)}, s32[3,2]{1,0:T(4,128)S(1)}, u32[]{:S(2)}) copy-start(s32[3,2]{1,0:T(4,128)S(1)} %copy.13.offsets) | copy-start | bytes 76
  162.1 4.0 %copy-start = (f32[6,512,256]{2,1,0:T(8,128)S(1)}, f32[6,512,256]{2,1,0:T(8,128)}, u32[]{:S(2)}) copy-start(f32[6,512,256]{2,1,0:T(8,128)} %get-tuple-element.25) | copy-start | bytes 9437188
